TPU v7x, 512 devices: a whole 4x8x8 slice. The times are simulated.
512 devices in a mesh: grp: 2 (over core), row: 8 (over y), col: 32 (over x, z).
Axes of the slice: x: 4, y: 8, z: 8, core: 2. Of those that a mesh axis runs over, the one named last changes fastest.
Arguments:
- v_pppp: bfloat16 [2, 12288, 12288], P('grp', 'col', 'row'), may hold values from -0.0546875 to 0.0546875
- lam: bfloat16 [2, 1280, 12288], P('grp', 'row', 'col'), may hold values from -6 to 6
- v_hhpp: bfloat16 [2, 1280, 12288], P('grp', 'col', 'row'), may hold values from -6 to 6
- hole_energy: float32 [2, 1280], P('grp', 'col'), may hold values from -3 to -1
- part_energy: float32 [2, 12288], P('grp', 'row'), may hold values from 0.5 to 3
- pp_dim: int32 [2], P('grp'), may hold values from 3072 to 12288, as said below
- hh_dim: int32 [2], P('grp'), may hold values from 320 to 1280, as said below
Outputs:
- new_lam: bfloat16 [2, 1280, 12288], P('grp', 'col', 'row')
Inputs may be any that keep to these rules, and one draw needn't show every extreme that they name: `pp_dim`: one channel, not always the same, uses all 12288 states; each uses at least a quarter of them. `hh_dim`: one channel, not always the same, uses all 1280 states; each uses at least a quarter of them.
All inputs are finite; a program needn't handle non-finite values.
Results may differ from a plain program's by a relative error of at most 0.019.
Values may be sent and summed in bfloat16 or wider, within the bound.
No kernel may reach another device: no remote copies, remote signals or barrier semaphores. Data moves between devices by JAX's collectives and lax.ppermute only.
A program may use at most 64 MiB of HBM per device.

v0:
```python
import jax
import jax.numpy as jnp
from jax import lax
from jax.sharding import PartitionSpec as P


def local(v_pppp, lam, v_hhpp, hole_energy, part_energy, pp_dim, hh_dim):
    pp_used = pp_dim[0]
    hh_used = hh_dim[0]
    hole_local = lam.shape[1]
    part_local = lam.shape[2]
    hole_start = lax.axis_index("row") * hole_local
    part_start = lax.axis_index("col") * part_local
    hole_ids = hole_start + jnp.arange(hole_local, dtype=jnp.int32)
    part_ids = part_start + jnp.arange(part_local, dtype=jnp.int32)
    keep = (hole_ids[:, None] < hh_used) & (part_ids[None, :] < pp_used)
    masked = jnp.where(keep[None], lam, jnp.zeros_like(lam))
    gathered = lax.all_gather(masked, "row", axis=1, tiled=True)
    left = gathered[0]
    tile = v_pppp[0]
    out_rows = v_hhpp.shape[1]
    out_cols = v_hhpp.shape[2]
    ladder = lax.psum_scatter(
        jnp.dot(left, tile, preferred_element_type=jnp.float32).astype(jnp.bfloat16),
        "col",
        scatter_dimension=0,
        tiled=True,
    ).astype(jnp.float32)
    out_hole = lax.axis_index("col") * out_rows + jnp.arange(out_rows, dtype=jnp.int32)
    out_part = lax.axis_index("row") * out_cols + jnp.arange(out_cols, dtype=jnp.int32)
    valid = (out_hole[:, None] < hh_used) & (out_part[None, :] < pp_used)
    denom = hole_energy[0][:, None] - part_energy[0][None, :]
    value = (v_hhpp[0].astype(jnp.float32) + ladder) / denom
    result = jnp.where(valid, value, jnp.zeros_like(value)).astype(jnp.bfloat16)
    return result[None]


def solution(mesh):
    return jax.shard_map(
        local,
        mesh=mesh,
        in_specs=(
            P("grp", "col", "row"),
            P("grp", "row", "col"),
            P("grp", "col", "row"),
            P("grp", "col"),
            P("grp", "row"),
            P("grp"),
            P("grp"),
        ),
        out_specs=P("grp", "col", "row"),
        check_vma=False,
    )
```

profile of v0, /device:TPU:56, one launch (start us, length us, event | category | flops | bytes accessed | tf_op | source)
XLA Modules:
  0.0 280.3 jit_solution(8383924701011226108)
XLA Ops:
  6.5 0.0 copy-start
  6.5 0.0 reduce-scatter.2.cloned.1.call-start
  8.0 1.0 and_select_fusion
  9.0 28.5 %all_gather.3 = bf16[1,1280,384]{2,1,0:T(8,128)(2,1)S(1)} all-gather(bf16[1,160,384]{2,1,0:T(8,128)(2,1)S(1)} %and_select_fusion), channel_id=1, replica_groups=mesh['grp'=2,'row'=8,'col'=32] {'row'}, dimensions={1}, use_global_device_ids=true | all-gather | bytes 1105920 | tf_op jit(solution)/shard_map/all_gather | solution.py:18
  37.5 0.0 copy-done
  37.5 4.1 %convolution_convert_fusion = bf16[1280,1536]{1,0:T(8,128)(2,1)} fusion(bf16[1,384,1536]{2,1,0:T(8,128)(2,1)S(1)} %copy-done, bf16[1,1280,384]{2,1,0:T(8,128)(2,1)S(1)} %all_gather.3), kind=kOutput, calls=%fused_computation | convolution fusion | flops 1511915520 | bytes 6094848 | tf_op jit(solution)/shard_map/dot_general | solution.py:24
  41.5 0.0 copy-start.2
  41.5 0.0 copy-start.1
  41.6 0.0 copy-start.3
  41.6 0.0 reduce-scatter.2.cloned.1.call-update
  41.6 0.7 copy-done.2
  42.3 229.5 %reduce-scatter.2.cloned.1.call-done = bf16[40,1536]{1,0:T(8,128)(2,1)} async-done(((bf16[1280,1536]{1,0:T(8,128)(2,1)}), bf16[40,1536]{1,0:T(8,128)(2,1)}) %reduce-scatter.2.cloned.1.call-update) | async-done | bytes 122896 | tf_op jit(solution)/shard_map/reduce_scatter | solution.py:23
  271.8 0.0 copy-done.1
  271.8 0.0 copy-done.3
  271.8 1.7 fusion.5
  (5 shorter events, 0.1 us)
Async XLA Ops:
  6.5 30.9 %copy-start = (bf16[1,384,1536]{2,1,0:T(8,128)(2,1)S(1)}, bf16[1,384,1536]{2,1,0:T(8,128)(2,1)}, u32[]{:S(2)}) copy-start(bf16[1,384,1536]{2,1,0:T(8,128)(2,1)} %param.7) | copy-start | bytes 3538948
  6.5 265.3 %reduce-scatter.2.cloned.1.call-start = ((), (), s32[]{:S(2)}) async-start(), calls=%async_computation.1 | async-start | bytes 4055040 | tf_op jit(solution)/shard_map/reduce_scatter | solution.py:23
  41.5 0.7 copy-start.2
  41.5 230.2 %copy-start.1 = (bf16[1,40,1536]{2,1,0:T(8,128)(2,1)S(1)}, bf16[1,40,1536]{2,1,0:T(8,128)(2,1)}, u32[]{:S(2)}) copy-start(bf16[1,40,1536]{2,1,0:T(8,128)(2,1)} %param.9) | copy-start | bytes 368644
  41.6 230.2 %copy-start.3 = (f32[1,40]{1,0:T(1,128)S(1)}, f32[1,40]{1,0:T(1,128)}, u32[]{:S(2)}) copy-start(f32[1,40]{1,0:T(1,128)} %param.10) | copy-start | bytes 484
Sparse Core Ops, SparseCore 0:
  41.7 230.0 reduce-scatter.1
where the time goes:
time: 281 us; the launch traced here: 280 us
  waiting for transfers between devices  230 us (82%)
  blocking collectives  28.5 us (10%)
  between operations  14.8 us (5%)
  matrix products  4.09 us (1%)
    reduce_scatter x1, waiting for transfers between devices, local(): lax.psum_scatter(jnp.dot(left, tile, preferred_element_type=jnp.float32)....  229 us
    all_gather x1, blocking collectives, local(): gathered = lax.all_gather(masked, 'row', axis=1, tiled=True)  28.5 us
  transfers between devices with their start and end apart: 1, of which 1 were waited for; matrix products, arithmetic and copies ran while one was open for 0% of the time, Pallas kernels for 0%

commit v1 on v0

v1 whole, which is shorter than its diff:
```python
import jax
import jax.numpy as jnp
from jax import lax
from jax.sharding import PartitionSpec as P

NX, NZ, NY = 4, 8, 8


def ring_perm(axis, step):
    if axis == "y":
        return [(i, (i + step) % NY) for i in range(NY)]
    pairs = []
    for x in range(NX):
        for z in range(NZ):
            if axis == "x":
                pairs.append((x * NZ + z, ((x + step) % NX) * NZ + z))
            else:
                pairs.append((x * NZ + z, x * NZ + (z + step) % NZ))
    return pairs


def send(value, axis, step):
    return lax.ppermute(value, "row" if axis == "y" else "col", ring_perm(axis, step))


def gather_rows(shard, me):
    half = shard.shape[0] // 2
    out = jnp.zeros((NY,) + shard.shape, shard.dtype)
    put = lambda out, value, at, row: lax.dynamic_update_slice(out, value[None], (at % NY, row, 0))
    out = put(out, shard, me, 0)
    up = down = shard
    for s in range(1, NY // 2):
        up = send(up, "y", 1)
        down = send(down, "y", -1)
        out = put(out, up, me - s + NY, 0)
        out = put(out, down, me + s, 0)
    up = send(up[:half], "y", 1)
    down = send(down[half:], "y", -1)
    out = put(out, up, me + NY // 2, 0)
    out = put(out, down, me + NY // 2, half)
    return out


def ring_reduce(axis, size, me, part):
    far = size // 2
    up = send(part((me + far) % size, 0, 1).astype(jnp.bfloat16), axis, 1)
    down = send(part((me + far) % size, 1, 2).astype(jnp.bfloat16), axis, -1)
    for s in range(far - 1, 0, -1):
        mine_up = part((me + s) % size, 0, 2)
        mine_down = part((me - s + size) % size, 0, 2)
        if s == far - 1:
            up = jnp.concatenate([up, jnp.zeros_like(up)], axis=-1)
            down = jnp.concatenate([jnp.zeros_like(down), down], axis=-1)
        up = send((mine_up + up.astype(jnp.float32)).astype(jnp.bfloat16), axis, 1)
        down = send((mine_down + down.astype(jnp.float32)).astype(jnp.bfloat16), axis, -1)
    return part(me, 0, 2) + up.astype(jnp.float32) + down.astype(jnp.float32)


def local(v_pppp, lam, v_hhpp, hole_energy, part_energy, pp_dim, hh_dim):
    pp_used = pp_dim[0]
    hh_used = hh_dim[0]
    hole_local = lam.shape[1]
    part_local = lam.shape[2]
    y = lax.axis_index("row")
    col = lax.axis_index("col")
    x, z = col // NZ, col % NZ
    hole_ids = y * hole_local + jnp.arange(hole_local, dtype=jnp.int32)
    part_ids = col * part_local + jnp.arange(part_local, dtype=jnp.int32)
    keep = (hole_ids[:, None] < hh_used) & (part_ids[None, :] < pp_used)
    masked = jnp.where(keep, lam[0], jnp.zeros_like(lam[0]))
    out_rows = v_hhpp.shape[1]
    out_cols = v_hhpp.shape[2]
    left = gather_rows(masked, y).reshape(NX, NZ, out_rows, part_local)
    tile = v_pppp[0]
    mid = out_cols // 2
    dot = lambda a, b: jnp.dot(a, b, preferred_element_type=jnp.float32)

    def z_term(owner, lo, hi):
        rows = lax.dynamic_slice_in_dim(left, owner, 1, 1).reshape(NX * out_rows, part_local)
        return dot(rows, tile[:, lo * (mid // 2) : hi * (mid // 2)])

    def x_term(owner, lo, hi):
        rows = lax.dynamic_slice_in_dim(left, owner, 1, 0).reshape(NZ * out_rows, part_local)
        return dot(rows, tile[:, mid + lo * (mid // 2) : mid + hi * (mid // 2)])

    by_z = ring_reduce("z", NZ, z, z_term).reshape(NX, out_rows, mid)
    by_x = ring_reduce("x", NX, x, x_term).reshape(NZ, out_rows, mid)

    def rest_of(parts):
        def term(owner, lo, hi):
            block = lax.dynamic_slice_in_dim(parts, owner, 1, 0)[0]
            return block[:, lo * (mid // 2) : hi * (mid // 2)]

        return term

    first = ring_reduce("x", NX, x, rest_of(by_z))
    second = ring_reduce("z", NZ, z, rest_of(by_x))
    ladder = jnp.concatenate([first, second], axis=1)
    out_hole = col * out_rows + jnp.arange(out_rows, dtype=jnp.int32)
    out_part = y * out_cols + jnp.arange(out_cols, dtype=jnp.int32)
    valid = (out_hole[:, None] < hh_used) & (out_part[None, :] < pp_used)
    denom = hole_energy[0][:, None] - part_energy[0][None, :]
    value = (v_hhpp[0].astype(jnp.float32) + ladder) / denom
    result = jnp.where(valid, value, jnp.zeros_like(value)).astype(jnp.bfloat16)
    return result[None]


def solution(mesh):
    return jax.shard_map(
        local,
        mesh=mesh,
        in_specs=(
            P("grp", "col", "row"),
            P("grp", "row", "col"),
            P("grp", "col", "row"),
            P("grp", "col"),
            P("grp", "row"),
            P("grp"),
            P("grp"),
        ),
        out_specs=P("grp", "col", "row"),
        check_vma=False,
    )
```

time: 281 us -> 145 us (0.52)
  the two profiles are of different devices: /device:TPU:56 before, /device:TPU:24 now
where the time goes in v1:
time: 145 us; the launch traced here: 144 us
  starting transfers between devices  113 us (78%)
  waiting for transfers between devices  20.5 us (14%)
  matrix products  4.38 us (3%)
  other arithmetic  2.53 us (2%)
  between operations  2.52 us (2%)
    ppermute x32, starting transfers between devices, send(): lax.ppermute(value, 'row' if axis == 'y' else 'col', ring_perm(axis, step))  113 us
    ppermute x32, waiting for transfers between devices, send(): lax.ppermute(value, 'row' if axis == 'y' else 'col', ring_perm(axis, step))  20.5 us
    dot_general x14, matrix products, local(): dot = lambda a, b: jnp.dot(a, b, preferred_element_type=jnp.float32)  4.38 us
  transfers between devices with their start and end apart: 32, of which 7 were waited for; matrix products, arithmetic and copies ran while one was open for 3% of the time, Pallas kernels for 0%

profile of v1, /device:TPU:24, one launch (start us, length us, event | category | flops | bytes accessed | tf_op | source)
XLA Modules:
  0.0 143.6 jit_solution(634544601704218016)
XLA Ops:
  1.4 1.0 and_select_fusion
  2.4 4.7 %collective-permute-start = (bf16[160,384]{1,0:T(8,128)(2,1)S(1)}, bf16[160,384]{1,0:T(8,128)(2,1)S(1)}, u32[]{:S(2)}, u32[]{:S(2)}) collective-permute-start(bf16[160,384]{1,0:T(8,128)(2,1)S(1)} %and_select_fusion), channel_id=1, source_target_pairs={{0,32},{32,64},{64,96},{96,128},{128,160},{160,192},{192,224},{224... | collective-permute-start | bytes 368648 | tf_op jit(solution)/shard_map/ppermute | solution.py:23
  7.1 1.9 %collective-permute-start.1 = (bf16[160,384]{1,0:T(8,128)(2,1)S(1)}, bf16[160,384]{1,0:T(8,128)(2,1)S(1)}, u32[]{:S(2)}, u32[]{:S(2)}) collective-permute-start(bf16[160,384]{1,0:T(8,128)(2,1)S(1)} %and_select_fusion), channel_id=1, source_target_pairs={{0,224},{32,0},{64,32},{96,64},{128,96},{160,128},{192,160},{224,1... | collective-permute-start | bytes 368648 | tf_op jit(solution)/shard_map/ppermute | solution.py:23
  9.1 0.1 broadcast_in_dim.36
  9.2 0.1 fusion.35
  9.7 5.5 %collective-permute-start.2 = (bf16[160,384]{1,0:T(8,128)(2,1)S(1)}, bf16[160,384]{1,0:T(8,128)(2,1)S(1)}, u32[]{:S(2)}, u32[]{:S(2)}) collective-permute-start(bf16[160,384]{1,0:T(8,128)(2,1)S(1)} %collective-permute-done), channel_id=1, source_target_pairs={{0,32},{32,64},{64,96},{96,128},{128,160},{160,192},{192,224},{224... | collective-permute-start | bytes 368648 | tf_op jit(solution)/shard_map/ppermute | solution.py:23
  15.3 1.9 %collective-permute-start.3 = (bf16[160,384]{1,0:T(8,128)(2,1)S(1)}, bf16[160,384]{1,0:T(8,128)(2,1)S(1)}, u32[]{:S(2)}, u32[]{:S(2)}) collective-permute-start(bf16[160,384]{1,0:T(8,128)(2,1)S(1)} %collective-permute-done.1), channel_id=1, source_target_pairs={{0,224},{32,0},{64,32},{96,64},{128,96},{160,128},{192,160},{224,1... | collective-permute-start | bytes 368648 | tf_op jit(solution)/shard_map/ppermute | solution.py:23
  17.2 0.4 collective-permute-done.2
  17.7 5.5 %collective-permute-start.4 = (bf16[160,384]{1,0:T(8,128)(2,1)S(1)}, bf16[160,384]{1,0:T(8,128)(2,1)S(1)}, u32[]{:S(2)}, u32[]{:S(2)}) collective-permute-start(bf16[160,384]{1,0:T(8,128)(2,1)S(1)} %collective-permute-done.2), channel_id=1, source_target_pairs={{0,32},{32,64},{64,96},{96,128},{128,160},{160,192},{192,224},{224... | collective-permute-start | bytes 368648 | tf_op jit(solution)/shard_map/ppermute | solution.py:23
  23.2 0.0 collective-permute-done.3
  23.2 1.9 %collective-permute-start.5 = (bf16[160,384]{1,0:T(8,128)(2,1)S(1)}, bf16[160,384]{1,0:T(8,128)(2,1)S(1)}, u32[]{:S(2)}, u32[]{:S(2)}) collective-permute-start(bf16[160,384]{1,0:T(8,128)(2,1)S(1)} %collective-permute-done.3), channel_id=1, source_target_pairs={{0,224},{32,0},{64,32},{96,64},{128,96},{160,128},{192,160},{224,1... | collective-permute-start | bytes 368648 | tf_op jit(solution)/shard_map/ppermute | solution.py:23
  25.2 0.4 collective-permute-done.4
  25.6 5.5 %collective-permute-start.6 = (bf16[80,384]{1,0:T(8,128)(2,1)S(1)}, bf16[80,384]{1,0:T(8,128)(2,1)S(1)}, u32[]{:S(2)}, u32[]{:S(2)}) collective-permute-start(bf16[80,384]{1,0:T(8,128)(2,1)S(1)} %slice.60), channel_id=1, source_target_pairs={{0,32},{32,64},{64,96},{96,128},{128,160},{160,192},{192,224},{224... | collective-permute-start | bytes 184328 | tf_op jit(solution)/shard_map/ppermute | solution.py:23
  31.2 0.0 collective-permute-done.5
  31.2 1.9 %collective-permute-start.7 = (bf16[80,384]{1,0:T(8,128)(2,1)S(1)}, bf16[80,384]{1,0:T(8,128)(2,1)S(1)}, u32[]{:S(2)}, u32[]{:S(2)}) collective-permute-start(bf16[80,384]{1,0:T(8,128)(2,1)S(1)} %slice.61), channel_id=1, source_target_pairs={{0,224},{32,0},{64,32},{96,64},{128,96},{160,128},{192,160},{224,1... | collective-permute-start | bytes 184328 | tf_op jit(solution)/shard_map/ppermute | solution.py:23
  33.3 5.3 %collective-permute-done.7 = bf16[80,384]{1,0:T(8,128)(2,1)S(1)} collective-permute-done((bf16[80,384]{1,0:T(8,128)(2,1)S(1)}, bf16[80,384]{1,0:T(8,128)(2,1)S(1)}, u32[]{:S(2)}, u32[]{:S(2)}) %collective-permute-start.7) | collective-permute-done | bytes 61472 | tf_op jit(solution)/shard_map/ppermute | solution.py:23
  38.6 0.1 constant_dynamic-slice_fusion.8
  38.7 0.2 convolution_convert_fusion.3
  38.9 0.2 convolution_convert_fusion.2
  39.2 0.1 constant_dynamic-slice_fusion.2
  39.3 0.3 convolution_convert_fusion.1
  39.6 0.3 convolution_convert_fusion
  40.0 4.3 %collective-permute-start.8 = (bf16[160,384]{1,0:T(8,128)(2,1)S(1)}, bf16[160,384]{1,0:T(8,128)(2,1)S(1)}, u32[]{:S(2)}, u32[]{:S(2)}) collective-permute-start(bf16[160,384]{1,0:T(8,128)(2,1)S(1)} %convolution_convert_fusion.3), channel_id=1, source_target_pairs={{0,1},{1,2},{2,3},{3,4},{4,5},{5,6},{6,7},{7,0},{8,9},{9,10},{10,1... | collective-permute-start | bytes 368648 | tf_op jit(solution)/shard_map/ppermute | solution.py:23
  44.3 0.3 fusion.25
  44.5 0.3 fusion.27
  44.8 8.6 %collective-permute-start.12 = (bf16[160,384]{1,0:T(8,128)(2,1)S(1)}, bf16[160,384]{1,0:T(8,128)(2,1)S(1)}, u32[]{:S(2)}, u32[]{:S(2)}) collective-permute-start(bf16[160,384]{1,0:T(8,128)(2,1)S(1)} %convolution_convert_fusion.2), channel_id=1, source_target_pairs={{0,7},{1,0},{2,1},{3,2},{4,3},{5,4},{6,5},{7,6},{8,15},{9,8},{10,9... | collective-permute-start | bytes 368648 | tf_op jit(solution)/shard_map/ppermute | solution.py:23
  53.4 0.3 fusion.21
  53.7 3.4 %collective-permute-start.20 = (bf16[320,384]{1,0:T(8,128)(2,1)S(1)}, bf16[320,384]{1,0:T(8,128)(2,1)S(1)}, u32[]{:S(2)}, u32[]{:S(2)}) collective-permute-start(bf16[320,384]{1,0:T(8,128)(2,1)S(1)} %convolution_convert_fusion.1), channel_id=1, source_target_pairs={{0,8},{1,9},{2,10},{3,11},{4,12},{5,13},{6,14},{7,15},{8,16},{9,17... | collective-permute-start | bytes 737288 | tf_op jit(solution)/shard_map/ppermute | solution.py:23
  57.1 3.7 %collective-permute-start.22 = (bf16[320,384]{1,0:T(8,128)(2,1)S(1)}, bf16[320,384]{1,0:T(8,128)(2,1)S(1)}, u32[]{:S(2)}, u32[]{:S(2)}) collective-permute-start(bf16[320,384]{1,0:T(8,128)(2,1)S(1)} %convolution_convert_fusion), channel_id=1, source_target_pairs={{0,24},{1,25},{2,26},{3,27},{4,28},{5,29},{6,30},{7,31},{8,0},{9,1... | collective-permute-start | bytes 737288 | tf_op jit(solution)/shard_map/ppermute | solution.py:23
  60.8 0.4 fusion.4
  61.2 0.3 fusion.19
  61.5 0.3 add_convert_fusion.7
  61.8 1.9 %collective-permute-start.9 = (bf16[160,768]{1,0:T(8,128)(2,1)S(1)}, bf16[160,768]{1,0:T(8,128)(2,1)S(1)}, u32[]{:S(2)}, u32[]{:S(2)}) collective-permute-start(bf16[160,768]{1,0:T(8,128)(2,1)S(1)} %add_convert_fusion.7), channel_id=1, source_target_pairs={{0,1},{1,2},{2,3},{3,4},{4,5},{5,6},{6,7},{7,0},{8,9},{9,10},{10,1... | collective-permute-start | bytes 737288 | tf_op jit(solution)/shard_map/ppermute | solution.py:23
  63.7 0.3 add_convert_fusion.4
  64.0 5.1 %collective-permute-start.13 = (bf16[160,768]{1,0:T(8,128)(2,1)S(1)}, bf16[160,768]{1,0:T(8,128)(2,1)S(1)}, u32[]{:S(2)}, u32[]{:S(2)}) collective-permute-start(bf16[160,768]{1,0:T(8,128)(2,1)S(1)} %add_convert_fusion.4), channel_id=1, source_target_pairs={{0,7},{1,0},{2,1},{3,2},{4,3},{5,4},{6,5},{7,6},{8,15},{9,8},{10,9... | collective-permute-start | bytes 737288 | tf_op jit(solution)/shard_map/ppermute | solution.py:23
  69.2 0.4 add_convert_fusion.1
  69.6 2.2 %collective-permute-start.21 = (bf16[320,768]{1,0:T(8,128)(2,1)S(1)}, bf16[320,768]{1,0:T(8,128)(2,1)S(1)}, u32[]{:S(2)}, u32[]{:S(2)}) collective-permute-start(bf16[320,768]{1,0:T(8,128)(2,1)S(1)} %add_convert_fusion.1), channel_id=1, source_target_pairs={{0,8},{1,9},{2,10},{3,11},{4,12},{5,13},{6,14},{7,15},{8,16},{9,17... | collective-permute-start | bytes 1474568 | tf_op jit(solution)/shard_map/ppermute | solution.py:23
  71.8 0.4 add_convert_fusion
  72.2 4.9 %collective-permute-start.23 = (bf16[320,768]{1,0:T(8,128)(2,1)S(1)}, bf16[320,768]{1,0:T(8,128)(2,1)S(1)}, u32[]{:S(2)}, u32[]{:S(2)}) collective-permute-start(bf16[320,768]{1,0:T(8,128)(2,1)S(1)} %add_convert_fusion), channel_id=1, source_target_pairs={{0,24},{1,25},{2,26},{3,27},{4,28},{5,29},{6,30},{7,31},{8,0},{9,1... | collective-permute-start | bytes 1474568 | tf_op jit(solution)/shard_map/ppermute | solution.py:23
  77.2 1.9 %collective-permute-start.10 = (bf16[160,768]{1,0:T(8,128)(2,1)S(1)}, bf16[160,768]{1,0:T(8,128)(2,1)S(1)}, u32[]{:S(2)}, u32[]{:S(2)}) collective-permute-start(bf16[160,768]{1,0:T(8,128)(2,1)S(1)} %add_convert_fusion.6), channel_id=1, source_target_pairs={{0,1},{1,2},{2,3},{3,4},{4,5},{5,6},{6,7},{7,0},{8,9},{9,10},{10,1... | collective-permute-start | bytes 737288 | tf_op jit(solution)/shard_map/ppermute | solution.py:23
  79.2 5.1 %collective-permute-start.14 = (bf16[160,768]{1,0:T(8,128)(2,1)S(1)}, bf16[160,768]{1,0:T(8,128)(2,1)S(1)}, u32[]{:S(2)}, u32[]{:S(2)}) collective-permute-start(bf16[160,768]{1,0:T(8,128)(2,1)S(1)} %add_convert_fusion.3), channel_id=1, source_target_pairs={{0,7},{1,0},{2,1},{3,2},{4,3},{5,4},{6,5},{7,6},{8,15},{9,8},{10,9... | collective-permute-start | bytes 737288 | tf_op jit(solution)/shard_map/ppermute | solution.py:23
  84.3 4.0 %collective-permute-done.10 = bf16[160,768]{1,0:T(8,128)(2,1)S(1)} collective-permute-done((bf16[160,768]{1,0:T(8,128)(2,1)S(1)}, bf16[160,768]{1,0:T(8,128)(2,1)S(1)}, u32[]{:S(2)}, u32[]{:S(2)}) %collective-permute-start.10) | collective-permute-done | bytes 245792 | tf_op jit(solution)/shard_map/ppermute | solution.py:23
  88.4 1.9 %collective-permute-start.11 = (bf16[160,768]{1,0:T(8,128)(2,1)S(1)}, bf16[160,768]{1,0:T(8,128)(2,1)S(1)}, u32[]{:S(2)}, u32[]{:S(2)}) collective-permute-start(bf16[160,768]{1,0:T(8,128)(2,1)S(1)} %add_convert_fusion.5), channel_id=1, source_target_pairs={{0,1},{1,2},{2,3},{3,4},{4,5},{5,6},{6,7},{7,0},{8,9},{9,10},{10,1... | collective-permute-start | bytes 737288 | tf_op jit(solution)/shard_map/ppermute | solution.py:23
  90.3 0.1 convert_add_fusion
  90.5 1.9 %collective-permute-start.24 = (bf16[40,384]{1,0:T(8,128)(2,1)S(1)}, bf16[40,384]{1,0:T(8,128)(2,1)S(1)}, u32[]{:S(2)}, u32[]{:S(2)}) collective-permute-start(bf16[40,384]{1,0:T(8,128)(2,1)S(1)} %get-tuple-element.23), channel_id=1, source_target_pairs={{0,1},{1,2},{2,3},{3,4},{4,5},{5,6},{6,7},{7,0},{8,9},{9,10},{10,1... | collective-permute-start | bytes 92168 | tf_op jit(solution)/shard_map/ppermute | solution.py:23
  92.4 0.1 add_convert_fusion.2
  92.5 5.1 %collective-permute-start.15 = (bf16[160,768]{1,0:T(8,128)(2,1)S(1)}, bf16[160,768]{1,0:T(8,128)(2,1)S(1)}, u32[]{:S(2)}, u32[]{:S(2)}) collective-permute-start(bf16[160,768]{1,0:T(8,128)(2,1)S(1)} %add_convert_fusion.2), channel_id=1, source_target_pairs={{0,7},{1,0},{2,1},{3,2},{4,3},{5,4},{6,5},{7,6},{8,15},{9,8},{10,9... | collective-permute-start | bytes 737288 | tf_op jit(solution)/shard_map/ppermute | solution.py:23
  97.6 0.9 collective-permute-done.24
  98.6 1.9 %collective-permute-start.25 = (bf16[40,768]{1,0:T(8,128)(2,1)S(1)}, bf16[40,768]{1,0:T(8,128)(2,1)S(1)}, u32[]{:S(2)}, u32[]{:S(2)}) collective-permute-start(bf16[40,768]{1,0:T(8,128)(2,1)S(1)} %fusion.39), channel_id=1, source_target_pairs={{0,1},{1,2},{2,3},{3,4},{4,5},{5,6},{6,7},{7,0},{8,9},{9,10},{10,1... | collective-permute-start | bytes 184328 | tf_op jit(solution)/shard_map/ppermute | solution.py:23
  100.5 0.3 fusion.29
  100.8 5.1 %collective-permute-start.28 = (bf16[40,384]{1,0:T(8,128)(2,1)S(1)}, bf16[40,384]{1,0:T(8,128)(2,1)S(1)}, u32[]{:S(2)}, u32[]{:S(2)}) collective-permute-start(bf16[40,384]{1,0:T(8,128)(2,1)S(1)} %get-tuple-element.24), channel_id=1, source_target_pairs={{0,7},{1,0},{2,1},{3,2},{4,3},{5,4},{6,5},{7,6},{8,15},{9,8},{10,9... | collective-permute-start | bytes 92168 | tf_op jit(solution)/shard_map/ppermute | solution.py:23
  106.0 1.9 %collective-permute-start.26 = (bf16[40,768]{1,0:T(8,128)(2,1)S(1)}, bf16[40,768]{1,0:T(8,128)(2,1)S(1)}, u32[]{:S(2)}, u32[]{:S(2)}) collective-permute-start(bf16[40,768]{1,0:T(8,128)(2,1)S(1)} %fusion.40), channel_id=1, source_target_pairs={{0,1},{1,2},{2,3},{3,4},{4,5},{5,6},{6,7},{7,0},{8,9},{9,10},{10,1... | collective-permute-start | bytes 184328 | tf_op jit(solution)/shard_map/ppermute | solution.py:23
  108.0 0.1 convert_add_fusion.1
  108.1 5.2 %collective-permute-done.26 = bf16[40,768]{1,0:T(8,128)(2,1)S(1)} collective-permute-done((bf16[40,768]{1,0:T(8,128)(2,1)S(1)}, bf16[40,768]{1,0:T(8,128)(2,1)S(1)}, u32[]{:S(2)}, u32[]{:S(2)}) %collective-permute-start.26) | collective-permute-done | bytes 61472 | tf_op jit(solution)/shard_map/ppermute | solution.py:23
  113.4 1.9 %collective-permute-start.29 = (bf16[40,768]{1,0:T(8,128)(2,1)S(1)}, bf16[40,768]{1,0:T(8,128)(2,1)S(1)}, u32[]{:S(2)}, u32[]{:S(2)}) collective-permute-start(bf16[40,768]{1,0:T(8,128)(2,1)S(1)} %get-tuple-element.14), channel_id=1, source_target_pairs={{0,7},{1,0},{2,1},{3,2},{4,3},{5,4},{6,5},{7,6},{8,15},{9,8},{10,9... | collective-permute-start | bytes 184328 | tf_op jit(solution)/shard_map/ppermute | solution.py:23
  115.3 1.9 %collective-permute-start.16 = (bf16[40,384]{1,0:T(8,128)(2,1)S(1)}, bf16[40,384]{1,0:T(8,128)(2,1)S(1)}, u32[]{:S(2)}, u32[]{:S(2)}) collective-permute-start(bf16[40,384]{1,0:T(8,128)(2,1)S(1)} %get-tuple-element.21), channel_id=1, source_target_pairs={{0,8},{1,9},{2,10},{3,11},{4,12},{5,13},{6,14},{7,15},{8,16},{9,17... | collective-permute-start | bytes 92168 | tf_op jit(solution)/shard_map/ppermute | solution.py:23
  117.2 5.1 %collective-permute-start.18 = (bf16[40,384]{1,0:T(8,128)(2,1)S(1)}, bf16[40,384]{1,0:T(8,128)(2,1)S(1)}, u32[]{:S(2)}, u32[]{:S(2)}) collective-permute-start(bf16[40,384]{1,0:T(8,128)(2,1)S(1)} %get-tuple-element.22), channel_id=1, source_target_pairs={{0,24},{1,25},{2,26},{3,27},{4,28},{5,29},{6,30},{7,31},{8,0},{9,1... | collective-permute-start | bytes 92168 | tf_op jit(solution)/shard_map/ppermute | solution.py:23
  122.4 3.9 %collective-permute-start.27 = (bf16[40,768]{1,0:T(8,128)(2,1)S(1)}, bf16[40,768]{1,0:T(8,128)(2,1)S(1)}, u32[]{:S(2)}, u32[]{:S(2)}) collective-permute-start(bf16[40,768]{1,0:T(8,128)(2,1)S(1)} %get-tuple-element.13), channel_id=1, source_target_pairs={{0,1},{1,2},{2,3},{3,4},{4,5},{5,6},{6,7},{7,0},{8,9},{9,10},{10,1... | collective-permute-start | bytes 184328 | tf_op jit(solution)/shard_map/ppermute | solution.py:23
  126.3 3.1 %collective-permute-start.30 = (bf16[40,768]{1,0:T(8,128)(2,1)S(1)}, bf16[40,768]{1,0:T(8,128)(2,1)S(1)}, u32[]{:S(2)}, u32[]{:S(2)}) collective-permute-start(bf16[40,768]{1,0:T(8,128)(2,1)S(1)} %fusion.37), channel_id=1, source_target_pairs={{0,7},{1,0},{2,1},{3,2},{4,3},{5,4},{6,5},{7,6},{8,15},{9,8},{10,9... | collective-permute-start | bytes 184328 | tf_op jit(solution)/shard_map/ppermute | solution.py:23
  129.5 1.9 %collective-permute-start.17 = (bf16[40,768]{1,0:T(8,128)(2,1)S(1)}, bf16[40,768]{1,0:T(8,128)(2,1)S(1)}, u32[]{:S(2)}, u32[]{:S(2)}) collective-permute-start(bf16[40,768]{1,0:T(8,128)(2,1)S(1)} %get-tuple-element.19), channel_id=1, source_target_pairs={{0,8},{1,9},{2,10},{3,11},{4,12},{5,13},{6,14},{7,15},{8,16},{9,17... | collective-permute-start | bytes 184328 | tf_op jit(solution)/shard_map/ppermute | solution.py:23
  131.5 5.1 %collective-permute-start.19 = (bf16[40,768]{1,0:T(8,128)(2,1)S(1)}, bf16[40,768]{1,0:T(8,128)(2,1)S(1)}, u32[]{:S(2)}, u32[]{:S(2)}) collective-permute-start(bf16[40,768]{1,0:T(8,128)(2,1)S(1)} %get-tuple-element.20), channel_id=1, source_target_pairs={{0,24},{1,25},{2,26},{3,27},{4,28},{5,29},{6,30},{7,31},{8,0},{9,1... | collective-permute-start | bytes 184328 | tf_op jit(solution)/shard_map/ppermute | solution.py:23
  136.6 1.9 %collective-permute-start.31 = (bf16[40,768]{1,0:T(8,128)(2,1)S(1)}, bf16[40,768]{1,0:T(8,128)(2,1)S(1)}, u32[]{:S(2)}, u32[]{:S(2)}) collective-permute-start(bf16[40,768]{1,0:T(8,128)(2,1)S(1)} %fusion.38), channel_id=1, source_target_pairs={{0,7},{1,0},{2,1},{3,2},{4,3},{5,4},{6,5},{7,6},{8,15},{9,8},{10,9... | collective-permute-start | bytes 184328 | tf_op jit(solution)/shard_map/ppermute | solution.py:23
  138.6 4.1 %collective-permute-done.31 = bf16[40,768]{1,0:T(8,128)(2,1)S(1)} collective-permute-done((bf16[40,768]{1,0:T(8,128)(2,1)S(1)}, bf16[40,768]{1,0:T(8,128)(2,1)S(1)}, u32[]{:S(2)}, u32[]{:S(2)}) %collective-permute-start.31) | collective-permute-done | bytes 61472 | tf_op jit(solution)/shard_map/ppermute | solution.py:23
  142.8 0.8 fusion.16
  (63 shorter events, 0.7 us)
Async XLA Ops:
  0.0 9.2 %copy-start.1 = (bf16[1,160,384]{2,1,0:T(8,128)(2,1)S(1)}, bf16[1,160,384]{2,1,0:T(8,128)(2,1)}, u32[]{:S(2)}) copy-start(bf16[1,160,384]{2,1,0:T(8,128)(2,1)} %param.8) | copy-start | bytes 368644
  0.0 9.6 %copy-start.3 = (f32[1,1536]{1,0:T(1,128)S(1)}, f32[1,1536]{1,0:T(1,128)}, u32[]{:S(2)}) copy-start(f32[1,1536]{1,0:T(1,128)} %param.11) | copy-start | bytes 18436
  2.4 7.3 %collective-permute-start = (bf16[160,384]{1,0:T(8,128)(2,1)S(1)}, bf16[160,384]{1,0:T(8,128)(2,1)S(1)}, u32[]{:S(2)}, u32[]{:S(2)}) collective-permute-start(bf16[160,384]{1,0:T(8,128)(2,1)S(1)} %and_select_fusion), channel_id=1, source_target_pairs={{0,32},{32,64},{64,96},{96,128},{128,160},{160,192},{192,224},{224... | collective-permute-start | bytes 368648 | tf_op jit(solution)/shard_map/ppermute | solution.py:23
  7.1 8.2 %collective-permute-start.1 = (bf16[160,384]{1,0:T(8,128)(2,1)S(1)}, bf16[160,384]{1,0:T(8,128)(2,1)S(1)}, u32[]{:S(2)}, u32[]{:S(2)}) collective-permute-start(bf16[160,384]{1,0:T(8,128)(2,1)S(1)} %and_select_fusion), channel_id=1, source_target_pairs={{0,224},{32,0},{64,32},{96,64},{128,96},{160,128},{192,160},{224,1... | collective-permute-start | bytes 368648 | tf_op jit(solution)/shard_map/ppermute | solution.py:23
  9.7 8.0 %collective-permute-start.2 = (bf16[160,384]{1,0:T(8,128)(2,1)S(1)}, bf16[160,384]{1,0:T(8,128)(2,1)S(1)}, u32[]{:S(2)}, u32[]{:S(2)}) collective-permute-start(bf16[160,384]{1,0:T(8,128)(2,1)S(1)} %collective-permute-done), channel_id=1, source_target_pairs={{0,32},{32,64},{64,96},{96,128},{128,160},{160,192},{192,224},{224... | collective-permute-start | bytes 368648 | tf_op jit(solution)/shard_map/ppermute | solution.py:23
  15.3 8.0 %collective-permute-start.3 = (bf16[160,384]{1,0:T(8,128)(2,1)S(1)}, bf16[160,384]{1,0:T(8,128)(2,1)S(1)}, u32[]{:S(2)}, u32[]{:S(2)}) collective-permute-start(bf16[160,384]{1,0:T(8,128)(2,1)S(1)} %collective-permute-done.1), channel_id=1, source_target_pairs={{0,224},{32,0},{64,32},{96,64},{128,96},{160,128},{192,160},{224,1... | collective-permute-start | bytes 368648 | tf_op jit(solution)/shard_map/ppermute | solution.py:23
  17.7 8.0 %collective-permute-start.4 = (bf16[160,384]{1,0:T(8,128)(2,1)S(1)}, bf16[160,384]{1,0:T(8,128)(2,1)S(1)}, u32[]{:S(2)}, u32[]{:S(2)}) collective-permute-start(bf16[160,384]{1,0:T(8,128)(2,1)S(1)} %collective-permute-done.2), channel_id=1, source_target_pairs={{0,32},{32,64},{64,96},{96,128},{128,160},{160,192},{192,224},{224... | collective-permute-start | bytes 368648 | tf_op jit(solution)/shard_map/ppermute | solution.py:23
  23.2 8.0 %collective-permute-start.5 = (bf16[160,384]{1,0:T(8,128)(2,1)S(1)}, bf16[160,384]{1,0:T(8,128)(2,1)S(1)}, u32[]{:S(2)}, u32[]{:S(2)}) collective-permute-start(bf16[160,384]{1,0:T(8,128)(2,1)S(1)} %collective-permute-done.3), channel_id=1, source_target_pairs={{0,224},{32,0},{64,32},{96,64},{128,96},{160,128},{192,160},{224,1... | collective-permute-start | bytes 368648 | tf_op jit(solution)/shard_map/ppermute | solution.py:23
  25.6 7.6 %collective-permute-start.6 = (bf16[80,384]{1,0:T(8,128)(2,1)S(1)}, bf16[80,384]{1,0:T(8,128)(2,1)S(1)}, u32[]{:S(2)}, u32[]{:S(2)}) collective-permute-start(bf16[80,384]{1,0:T(8,128)(2,1)S(1)} %slice.60), channel_id=1, source_target_pairs={{0,32},{32,64},{64,96},{96,128},{128,160},{160,192},{192,224},{224... | collective-permute-start | bytes 184328 | tf_op jit(solution)/shard_map/ppermute | solution.py:23
  31.2 7.3 %collective-permute-start.7 = (bf16[80,384]{1,0:T(8,128)(2,1)S(1)}, bf16[80,384]{1,0:T(8,128)(2,1)S(1)}, u32[]{:S(2)}, u32[]{:S(2)}) collective-permute-start(bf16[80,384]{1,0:T(8,128)(2,1)S(1)} %slice.61), channel_id=1, source_target_pairs={{0,224},{32,0},{64,32},{96,64},{128,96},{160,128},{192,160},{224,1... | collective-permute-start | bytes 184328 | tf_op jit(solution)/shard_map/ppermute | solution.py:23
  33.2 5.5 %copy-start = (bf16[1,384,1536]{2,1,0:T(8,128)(2,1)S(1)}, bf16[1,384,1536]{2,1,0:T(8,128)(2,1)}, u32[]{:S(2)}) copy-start(bf16[1,384,1536]{2,1,0:T(8,128)(2,1)} %param.7) | copy-start | bytes 3538948
  40.0 21.5 %collective-permute-start.8 = (bf16[160,384]{1,0:T(8,128)(2,1)S(1)}, bf16[160,384]{1,0:T(8,128)(2,1)S(1)}, u32[]{:S(2)}, u32[]{:S(2)}) collective-permute-start(bf16[160,384]{1,0:T(8,128)(2,1)S(1)} %convolution_convert_fusion.3), channel_id=1, source_target_pairs={{0,1},{1,2},{2,3},{3,4},{4,5},{5,6},{6,7},{7,0},{8,9},{9,10},{10,1... | collective-permute-start | bytes 368648 | tf_op jit(solution)/shard_map/ppermute | solution.py:23
  44.8 18.9 %collective-permute-start.12 = (bf16[160,384]{1,0:T(8,128)(2,1)S(1)}, bf16[160,384]{1,0:T(8,128)(2,1)S(1)}, u32[]{:S(2)}, u32[]{:S(2)}) collective-permute-start(bf16[160,384]{1,0:T(8,128)(2,1)S(1)} %convolution_convert_fusion.2), channel_id=1, source_target_pairs={{0,7},{1,0},{2,1},{3,2},{4,3},{5,4},{6,5},{7,6},{8,15},{9,8},{10,9... | collective-permute-start | bytes 368648 | tf_op jit(solution)/shard_map/ppermute | solution.py:23
  53.7 15.5 %collective-permute-start.20 = (bf16[320,384]{1,0:T(8,128)(2,1)S(1)}, bf16[320,384]{1,0:T(8,128)(2,1)S(1)}, u32[]{:S(2)}, u32[]{:S(2)}) collective-permute-start(bf16[320,384]{1,0:T(8,128)(2,1)S(1)} %convolution_convert_fusion.1), channel_id=1, source_target_pairs={{0,8},{1,9},{2,10},{3,11},{4,12},{5,13},{6,14},{7,15},{8,16},{9,17... | collective-permute-start | bytes 737288 | tf_op jit(solution)/shard_map/ppermute | solution.py:23
  57.1 14.7 %collective-permute-start.22 = (bf16[320,384]{1,0:T(8,128)(2,1)S(1)}, bf16[320,384]{1,0:T(8,128)(2,1)S(1)}, u32[]{:S(2)}, u32[]{:S(2)}) collective-permute-start(bf16[320,384]{1,0:T(8,128)(2,1)S(1)} %convolution_convert_fusion), channel_id=1, source_target_pairs={{0,24},{1,25},{2,26},{3,27},{4,28},{5,29},{6,30},{7,31},{8,0},{9,1... | collective-permute-start | bytes 737288 | tf_op jit(solution)/shard_map/ppermute | solution.py:23
  61.8 15.3 %collective-permute-start.9 = (bf16[160,768]{1,0:T(8,128)(2,1)S(1)}, bf16[160,768]{1,0:T(8,128)(2,1)S(1)}, u32[]{:S(2)}, u32[]{:S(2)}) collective-permute-start(bf16[160,768]{1,0:T(8,128)(2,1)S(1)} %add_convert_fusion.7), channel_id=1, source_target_pairs={{0,1},{1,2},{2,3},{3,4},{4,5},{5,6},{6,7},{7,0},{8,9},{9,10},{10,1... | collective-permute-start | bytes 737288 | tf_op jit(solution)/shard_map/ppermute | solution.py:23
  64.0 15.1 %collective-permute-start.13 = (bf16[160,768]{1,0:T(8,128)(2,1)S(1)}, bf16[160,768]{1,0:T(8,128)(2,1)S(1)}, u32[]{:S(2)}, u32[]{:S(2)}) collective-permute-start(bf16[160,768]{1,0:T(8,128)(2,1)S(1)} %add_convert_fusion.4), channel_id=1, source_target_pairs={{0,7},{1,0},{2,1},{3,2},{4,3},{5,4},{6,5},{7,6},{8,15},{9,8},{10,9... | collective-permute-start | bytes 737288 | tf_op jit(solution)/shard_map/ppermute | solution.py:23
  69.6 20.7 %collective-permute-start.21 = (bf16[320,768]{1,0:T(8,128)(2,1)S(1)}, bf16[320,768]{1,0:T(8,128)(2,1)S(1)}, u32[]{:S(2)}, u32[]{:S(2)}) collective-permute-start(bf16[320,768]{1,0:T(8,128)(2,1)S(1)} %add_convert_fusion.1), channel_id=1, source_target_pairs={{0,8},{1,9},{2,10},{3,11},{4,12},{5,13},{6,14},{7,15},{8,16},{9,17... | collective-permute-start | bytes 1474568 | tf_op jit(solution)/shard_map/ppermute | solution.py:23
  72.2 18.1 %collective-permute-start.23 = (bf16[320,768]{1,0:T(8,128)(2,1)S(1)}, bf16[320,768]{1,0:T(8,128)(2,1)S(1)}, u32[]{:S(2)}, u32[]{:S(2)}) collective-permute-start(bf16[320,768]{1,0:T(8,128)(2,1)S(1)} %add_convert_fusion), channel_id=1, source_target_pairs={{0,24},{1,25},{2,26},{3,27},{4,28},{5,29},{6,30},{7,31},{8,0},{9,1... | collective-permute-start | bytes 1474568 | tf_op jit(solution)/shard_map/ppermute | solution.py:23
  77.2 11.2 %collective-permute-start.10 = (bf16[160,768]{1,0:T(8,128)(2,1)S(1)}, bf16[160,768]{1,0:T(8,128)(2,1)S(1)}, u32[]{:S(2)}, u32[]{:S(2)}) collective-permute-start(bf16[160,768]{1,0:T(8,128)(2,1)S(1)} %add_convert_fusion.6), channel_id=1, source_target_pairs={{0,1},{1,2},{2,3},{3,4},{4,5},{5,6},{6,7},{7,0},{8,9},{9,10},{10,1... | collective-permute-start | bytes 737288 | tf_op jit(solution)/shard_map/ppermute | solution.py:23
  79.2 13.3 %collective-permute-start.14 = (bf16[160,768]{1,0:T(8,128)(2,1)S(1)}, bf16[160,768]{1,0:T(8,128)(2,1)S(1)}, u32[]{:S(2)}, u32[]{:S(2)}) collective-permute-start(bf16[160,768]{1,0:T(8,128)(2,1)S(1)} %add_convert_fusion.3), channel_id=1, source_target_pairs={{0,7},{1,0},{2,1},{3,2},{4,3},{5,4},{6,5},{7,6},{8,15},{9,8},{10,9... | collective-permute-start | bytes 737288 | tf_op jit(solution)/shard_map/ppermute | solution.py:23
  88.4 19.6 %collective-permute-start.11 = (bf16[160,768]{1,0:T(8,128)(2,1)S(1)}, bf16[160,768]{1,0:T(8,128)(2,1)S(1)}, u32[]{:S(2)}, u32[]{:S(2)}) collective-permute-start(bf16[160,768]{1,0:T(8,128)(2,1)S(1)} %add_convert_fusion.5), channel_id=1, source_target_pairs={{0,1},{1,2},{2,3},{3,4},{4,5},{5,6},{6,7},{7,0},{8,9},{9,10},{10,1... | collective-permute-start | bytes 737288 | tf_op jit(solution)/shard_map/ppermute | solution.py:23
  90.5 8.1 %collective-permute-start.24 = (bf16[40,384]{1,0:T(8,128)(2,1)S(1)}, bf16[40,384]{1,0:T(8,128)(2,1)S(1)}, u32[]{:S(2)}, u32[]{:S(2)}) collective-permute-start(bf16[40,384]{1,0:T(8,128)(2,1)S(1)} %get-tuple-element.23), channel_id=1, source_target_pairs={{0,1},{1,2},{2,3},{3,4},{4,5},{5,6},{6,7},{7,0},{8,9},{9,10},{10,1... | collective-permute-start | bytes 92168 | tf_op jit(solution)/shard_map/ppermute | solution.py:23
  92.5 15.4 %collective-permute-start.15 = (bf16[160,768]{1,0:T(8,128)(2,1)S(1)}, bf16[160,768]{1,0:T(8,128)(2,1)S(1)}, u32[]{:S(2)}, u32[]{:S(2)}) collective-permute-start(bf16[160,768]{1,0:T(8,128)(2,1)S(1)} %add_convert_fusion.2), channel_id=1, source_target_pairs={{0,7},{1,0},{2,1},{3,2},{4,3},{5,4},{6,5},{7,6},{8,15},{9,8},{10,9... | collective-permute-start | bytes 737288 | tf_op jit(solution)/shard_map/ppermute | solution.py:23
  98.6 7.4 %collective-permute-start.25 = (bf16[40,768]{1,0:T(8,128)(2,1)S(1)}, bf16[40,768]{1,0:T(8,128)(2,1)S(1)}, u32[]{:S(2)}, u32[]{:S(2)}) collective-permute-start(bf16[40,768]{1,0:T(8,128)(2,1)S(1)} %fusion.39), channel_id=1, source_target_pairs={{0,1},{1,2},{2,3},{3,4},{4,5},{5,6},{6,7},{7,0},{8,9},{9,10},{10,1... | collective-permute-start | bytes 184328 | tf_op jit(solution)/shard_map/ppermute | solution.py:23
  100.8 7.3 %collective-permute-start.28 = (bf16[40,384]{1,0:T(8,128)(2,1)S(1)}, bf16[40,384]{1,0:T(8,128)(2,1)S(1)}, u32[]{:S(2)}, u32[]{:S(2)}) collective-permute-start(bf16[40,384]{1,0:T(8,128)(2,1)S(1)} %get-tuple-element.24), channel_id=1, source_target_pairs={{0,7},{1,0},{2,1},{3,2},{4,3},{5,4},{6,5},{7,6},{8,15},{9,8},{10,9... | collective-permute-start | bytes 92168 | tf_op jit(solution)/shard_map/ppermute | solution.py:23
  106.0 7.3 %collective-permute-start.26 = (bf16[40,768]{1,0:T(8,128)(2,1)S(1)}, bf16[40,768]{1,0:T(8,128)(2,1)S(1)}, u32[]{:S(2)}, u32[]{:S(2)}) collective-permute-start(bf16[40,768]{1,0:T(8,128)(2,1)S(1)} %fusion.40), channel_id=1, source_target_pairs={{0,1},{1,2},{2,3},{3,4},{4,5},{5,6},{6,7},{7,0},{8,9},{9,10},{10,1... | collective-permute-start | bytes 184328 | tf_op jit(solution)/shard_map/ppermute | solution.py:23
  108.0 34.7 %copy-start.2 = (bf16[1,40,1536]{2,1,0:T(8,128)(2,1)S(1)}, bf16[1,40,1536]{2,1,0:T(8,128)(2,1)}, u32[]{:S(2)}) copy-start(bf16[1,40,1536]{2,1,0:T(8,128)(2,1)} %param.9) | copy-start | bytes 368644
  108.0 34.7 %copy-start.4 = (f32[1,40]{1,0:T(1,128)S(1)}, f32[1,40]{1,0:T(1,128)}, u32[]{:S(2)}) copy-start(f32[1,40]{1,0:T(1,128)} %param.10) | copy-start | bytes 484
  113.4 12.9 %collective-permute-start.29 = (bf16[40,768]{1,0:T(8,128)(2,1)S(1)}, bf16[40,768]{1,0:T(8,128)(2,1)S(1)}, u32[]{:S(2)}, u32[]{:S(2)}) collective-permute-start(bf16[40,768]{1,0:T(8,128)(2,1)S(1)} %get-tuple-element.14), channel_id=1, source_target_pairs={{0,7},{1,0},{2,1},{3,2},{4,3},{5,4},{6,5},{7,6},{8,15},{9,8},{10,9... | collective-permute-start | bytes 184328 | tf_op jit(solution)/shard_map/ppermute | solution.py:23
  115.3 14.2 %collective-permute-start.16 = (bf16[40,384]{1,0:T(8,128)(2,1)S(1)}, bf16[40,384]{1,0:T(8,128)(2,1)S(1)}, u32[]{:S(2)}, u32[]{:S(2)}) collective-permute-start(bf16[40,384]{1,0:T(8,128)(2,1)S(1)} %get-tuple-element.21), channel_id=1, source_target_pairs={{0,8},{1,9},{2,10},{3,11},{4,12},{5,13},{6,14},{7,15},{8,16},{9,17... | collective-permute-start | bytes 92168 | tf_op jit(solution)/shard_map/ppermute | solution.py:23
  117.2 12.3 %collective-permute-start.18 = (bf16[40,384]{1,0:T(8,128)(2,1)S(1)}, bf16[40,384]{1,0:T(8,128)(2,1)S(1)}, u32[]{:S(2)}, u32[]{:S(2)}) collective-permute-start(bf16[40,384]{1,0:T(8,128)(2,1)S(1)} %get-tuple-element.22), channel_id=1, source_target_pairs={{0,24},{1,25},{2,26},{3,27},{4,28},{5,29},{6,30},{7,31},{8,0},{9,1... | collective-permute-start | bytes 92168 | tf_op jit(solution)/shard_map/ppermute | solution.py:23
  122.4 16.2 %collective-permute-start.27 = (bf16[40,768]{1,0:T(8,128)(2,1)S(1)}, bf16[40,768]{1,0:T(8,128)(2,1)S(1)}, u32[]{:S(2)}, u32[]{:S(2)}) collective-permute-start(bf16[40,768]{1,0:T(8,128)(2,1)S(1)} %get-tuple-element.13), channel_id=1, source_target_pairs={{0,1},{1,2},{2,3},{3,4},{4,5},{5,6},{6,7},{7,0},{8,9},{9,10},{10,1... | collective-permute-start | bytes 184328 | tf_op jit(solution)/shard_map/ppermute | solution.py:23
  126.3 10.3 %collective-permute-start.30 = (bf16[40,768]{1,0:T(8,128)(2,1)S(1)}, bf16[40,768]{1,0:T(8,128)(2,1)S(1)}, u32[]{:S(2)}, u32[]{:S(2)}) collective-permute-start(bf16[40,768]{1,0:T(8,128)(2,1)S(1)} %fusion.37), channel_id=1, source_target_pairs={{0,7},{1,0},{2,1},{3,2},{4,3},{5,4},{6,5},{7,6},{8,15},{9,8},{10,9... | collective-permute-start | bytes 184328 | tf_op jit(solution)/shard_map/ppermute | solution.py:23
  129.5 9.0 %collective-permute-start.17 = (bf16[40,768]{1,0:T(8,128)(2,1)S(1)}, bf16[40,768]{1,0:T(8,128)(2,1)S(1)}, u32[]{:S(2)}, u32[]{:S(2)}) collective-permute-start(bf16[40,768]{1,0:T(8,128)(2,1)S(1)} %get-tuple-element.19), channel_id=1, source_target_pairs={{0,8},{1,9},{2,10},{3,11},{4,12},{5,13},{6,14},{7,15},{8,16},{9,17... | collective-permute-start | bytes 184328 | tf_op jit(solution)/shard_map/ppermute | solution.py:23
  131.5 7.1 %collective-permute-start.19 = (bf16[40,768]{1,0:T(8,128)(2,1)S(1)}, bf16[40,768]{1,0:T(8,128)(2,1)S(1)}, u32[]{:S(2)}, u32[]{:S(2)}) collective-permute-start(bf16[40,768]{1,0:T(8,128)(2,1)S(1)} %get-tuple-element.20), channel_id=1, source_target_pairs={{0,24},{1,25},{2,26},{3,27},{4,28},{5,29},{6,30},{7,31},{8,0},{9,1... | collective-permute-start | bytes 184328 | tf_op jit(solution)/shard_map/ppermute | solution.py:23
  136.6 6.1 %collective-permute-start.31 = (bf16[40,768]{1,0:T(8,128)(2,1)S(1)}, bf16[40,768]{1,0:T(8,128)(2,1)S(1)}, u32[]{:S(2)}, u32[]{:S(2)}) collective-permute-start(bf16[40,768]{1,0:T(8,128)(2,1)S(1)} %fusion.38), channel_id=1, source_target_pairs={{0,7},{1,0},{2,1},{3,2},{4,3},{5,4},{6,5},{7,6},{8,15},{9,8},{10,9... | collective-permute-start | bytes 184328 | tf_op jit(solution)/shard_map/ppermute | solution.py:23

commit v2 on v0

v2 whole, which is shorter than its diff:
```python
import jax
import jax.numpy as jnp
from jax import lax
from jax.sharding import Mesh, PartitionSpec as P

NX, NZ, NY = 4, 8, 8
COLS_A = 1024


def exchange_sum(parts, axis):
    got = lax.all_to_all(parts, axis, 0, 0)
    return jnp.sum(got.astype(jnp.float32), axis=0)


def local(v_pppp, lam, v_hhpp, hole_energy, part_energy, pp_dim, hh_dim):
    pp_used = pp_dim[0]
    hh_used = hh_dim[0]
    hole_local = lam.shape[1]
    part_local = lam.shape[2]
    y = lax.axis_index("row")
    col = lax.axis_index("x") * NZ + lax.axis_index("z")
    hole_ids = y * hole_local + jnp.arange(hole_local, dtype=jnp.int32)
    part_ids = col * part_local + jnp.arange(part_local, dtype=jnp.int32)
    keep = (hole_ids[:, None] < hh_used) & (part_ids[None, :] < pp_used)
    masked = jnp.where(keep, lam[0], jnp.zeros_like(lam[0]))
    out_rows = v_hhpp.shape[1]
    out_cols = v_hhpp.shape[2]
    left = lax.all_gather(masked, "row", axis=0, tiled=True)
    by_owner = left.reshape(NX, NZ, out_rows, part_local)
    left_z = by_owner.transpose(1, 0, 2, 3).reshape(NX * NZ * out_rows, part_local)
    tile = v_pppp[0]
    dot = lambda a, b: jnp.dot(a, b, preferred_element_type=jnp.float32).astype(jnp.bfloat16)

    part_a = dot(left_z, tile[:, :COLS_A])
    sum_a = lax.psum_scatter(part_a, "z", scatter_dimension=0, tiled=True)
    part_b = dot(left, tile[:, COLS_A:])
    cols_b = out_cols - COLS_A
    sum_b = exchange_sum(part_b.reshape(NX, NZ * out_rows, cols_b), "x").astype(jnp.bfloat16)
    ladder_b = exchange_sum(sum_b.reshape(NZ, out_rows, cols_b), "z")
    ladder_a = exchange_sum(sum_a.reshape(NX, out_rows, COLS_A), "x")
    ladder = jnp.concatenate([ladder_a, ladder_b], axis=1)

    out_hole = col * out_rows + jnp.arange(out_rows, dtype=jnp.int32)
    out_part = y * out_cols + jnp.arange(out_cols, dtype=jnp.int32)
    valid = (out_hole[:, None] < hh_used) & (out_part[None, :] < pp_used)
    denom = hole_energy[0][:, None] - part_energy[0][None, :]
    value = (v_hhpp[0].astype(jnp.float32) + ladder) / denom
    result = jnp.where(valid, value, jnp.zeros_like(value)).astype(jnp.bfloat16)
    return result[None]


def solution(mesh):
    split = Mesh(mesh.devices.reshape(2, NY, NX, NZ), ("grp", "row", "x", "z"))
    col = ("x", "z")
    return jax.shard_map(
        local,
        mesh=split,
        in_specs=(
            P("grp", col, "row"),
            P("grp", "row", col),
            P("grp", col, "row"),
            P("grp", col),
            P("grp", "row"),
            P("grp"),
            P("grp"),
        ),
        out_specs=P("grp", col, "row"),
        check_vma=False,
    )
```

time: 281 us -> 115 us (0.41)
  waiting for transfers between devices: 230 us -> 34.9 us
  blocking collectives: 28.5 us -> 43.3 us
  starting transfers between devices: 0.01 us -> 14.4 us
    reduce_scatter x1, waiting for transfers between devices: 229 us -> 13.1 us  [local(): sum_a = lax.psum_scatter(part_a, 'z', scatter_dimension=0, tiled=True)]
    all_to_all x0 -> x2, waiting for transfers between devices: none -> 21.8 us  [exchange_sum(): got = lax.all_to_all(parts, axis, 0, 0)]
    all_to_all x0 -> x1, blocking collectives: none -> 14.7 us  [exchange_sum(): got = lax.all_to_all(parts, axis, 0, 0)]
    all_to_all x0 -> x2, starting transfers between devices: none -> 14.4 us  [exchange_sum(): got = lax.all_to_all(parts, axis, 0, 0)]
  transfers between devices with their start and end apart: 1 -> 3, of which waited for: 1 -> 3; matrix products, arithmetic and copies ran while one was open for 0% -> 2% of each run, Pallas kernels for 0% -> 0%
where the time goes in v2:
time: 115 us; the launch traced here: 114 us
  blocking collectives  43.3 us (38%)
  waiting for transfers between devices  34.9 us (30%)
  between operations  14.8 us (13%)
  starting transfers between devices  14.4 us (13%)
  matrix products  3.86 us (3%)
  other arithmetic  2.93 us (3%)
    all_gather x1, blocking collectives, local(): left = lax.all_gather(masked, 'row', axis=0, tiled=True)  28.6 us
    all_to_all x2, waiting for transfers between devices, exchange_sum(): got = lax.all_to_all(parts, axis, 0, 0)  21.8 us
    all_to_all x1, blocking collectives, exchange_sum(): got = lax.all_to_all(parts, axis, 0, 0)  14.7 us
    all_to_all x2, starting transfers between devices, exchange_sum(): got = lax.all_to_all(parts, axis, 0, 0)  14.4 us
    reduce_scatter x1, waiting for transfers between devices, local(): sum_a = lax.psum_scatter(part_a, 'z', scatter_dimension=0, tiled=True)  13.1 us
    dot_general x2, matrix products, local(): jnp.dot(a, b, preferred_element_type=jnp.float32).astype(jnp.bfloat16)  3.86 us
  transfers between devices with their start and end apart: 3, of which 3 were waited for; matrix products, arithmetic and copies ran while one was open for 2% of the time, Pallas kernels for 0%

profile of v2, /device:TPU:56, one launch (start us, length us, event | category | flops | bytes accessed | tf_op | source)
XLA Modules:
  0.0 114.4 jit_solution(17872439864649378566)
XLA Ops:
  6.5 0.0 reduce-scatter.2.cloned.1.call-start
  7.9 1.0 and_select_fusion
  8.9 0.0 copy-start
  8.9 28.6 %all_gather.3 = bf16[1280,384]{1,0:T(8,128)(2,1)S(1)} all-gather(bf16[160,384]{1,0:T(8,128)(2,1)S(1)} %and_select_fusion), channel_id=1, replica_groups=mesh['grp'=2,'row'=8,'x'=4,'z'=8] {'row'}, dimensions={0}, use_global_device_ids=true | all-gather | bytes 1105920 | tf_op jit(solution)/shard_map/all_gather | solution.py:28
  37.5 0.1 copy.9
  37.6 0.0 copy-done
  37.6 3.0 %convolution_convert_fusion = bf16[1280,1024]{1,0:T(8,128)(2,1)} fusion(bf16[1280,384]{1,0:T(8,128)(2,1)S(1)} %bitcast.23, bf16[384,1536]{1,0:T(8,128)(2,1)S(1)} %bitcast.27), kind=kOutput, calls=%fused_computation | convolution fusion | flops 1007943680 | bytes 4390912 | tf_op jit(solution)/shard_map/dot_general | solution.py:32
  40.6 0.0 reduce-scatter.2.cloned.1.call-update
  40.7 0.8 convolution_convert_fusion.1
  41.5 14.7 %all_to_all.15 = bf16[4,320,512]{2,1,0:T(8,128)(2,1)S(1)} all-to-all(bf16[4,320,512]{2,1,0:T(8,128)(2,1)S(1)} %bitcast.22), channel_id=1, replica_groups=mesh['grp'=2,'row'=8,'x'=4,'z'=8] {'x'}, dimensions={0} | all-to-all | bytes 2621440 | tf_op jit(solution)/shard_map/all_to_all | solution.py:11
  56.2 0.0 copy-start.2
  56.2 1.0 reduce_sum.31
  57.2 0.0 copy-start.1
  57.2 0.0 copy-start.3
  57.2 10.4 %all-to-all-start.2 = ((bf16[8,40,512]{2,1,0:T(8,128)(2,1)}), bf16[8,40,512]{2,1,0:T(8,128)(2,1)S(1)}, u32[]{:S(2)}, u32[]{:S(2)}) async-start(bf16[8,40,512]{2,1,0:T(8,128)(2,1)} %bitcast.10), calls=%async_computation.3 | async-start | bytes 655360 | tf_op jit(solution)/shard_map/all_to_all | solution.py:11
  67.6 14.9 %all-to-all-done.2 = bf16[8,40,512]{2,1,0:T(8,128)(2,1)S(1)} async-done(((bf16[8,40,512]{2,1,0:T(8,128)(2,1)}), bf16[8,40,512]{2,1,0:T(8,128)(2,1)S(1)}, u32[]{:S(2)}, u32[]{:S(2)}) %all-to-all-start.2) | async-done | bytes 327712 | tf_op jit(solution)/shard_map/all_to_all | solution.py:11
  82.5 13.1 %reduce-scatter.2.cloned.1.call-done = bf16[160,1024]{1,0:T(8,128)(2,1)} async-done(((bf16[1280,1024]{1,0:T(8,128)(2,1)}), bf16[160,1024]{1,0:T(8,128)(2,1)}) %reduce-scatter.2.cloned.1.call-update) | async-done | bytes 327696 | tf_op jit(solution)/shard_map/reduce_scatter | solution.py:35
  95.6 4.0 %all-to-all-start = ((bf16[4,40,1024]{2,1,0:T(8,128)(2,1)}), bf16[4,40,1024]{2,1,0:T(8,128)(2,1)S(1)}, u32[]{:S(2)}, u32[]{:S(2)}) async-start(bf16[4,40,1024]{2,1,0:T(8,128)(2,1)} %bitcast.25), calls=%async_computation.1 | async-start | bytes 655360 | tf_op jit(solution)/shard_map/all_to_all | solution.py:11
  99.6 0.0 copy-done.2
  99.7 6.9 %all-to-all-done = bf16[4,40,1024]{2,1,0:T(8,128)(2,1)S(1)} async-done(((bf16[4,40,1024]{2,1,0:T(8,128)(2,1)}), bf16[4,40,1024]{2,1,0:T(8,128)(2,1)S(1)}, u32[]{:S(2)}, u32[]{:S(2)}) %all-to-all-start) | async-done | bytes 327712 | tf_op jit(solution)/shard_map/all_to_all | solution.py:11
  106.7 0.0 copy-done.1
  106.7 0.0 copy-done.3
  106.7 0.8 fusion.4
  (7 shorter events, 0.1 us)
Async XLA Ops:
  6.5 89.1 %reduce-scatter.2.cloned.1.call-start = ((), (), s32[]{:S(2)}) async-start(), calls=%async_computation.4 | async-start | bytes 2949120 | tf_op jit(solution)/shard_map/reduce_scatter | solution.py:35
  8.9 28.7 %copy-start = (bf16[1,384,1536]{2,1,0:T(8,128)(2,1)S(1)}, bf16[1,384,1536]{2,1,0:T(8,128)(2,1)}, u32[]{:S(2)}) copy-start(bf16[1,384,1536]{2,1,0:T(8,128)(2,1)} %param.7) | copy-start | bytes 3538948
  56.2 43.4 %copy-start.2 = (f32[1,1536]{1,0:T(1,128)S(1)}, f32[1,1536]{1,0:T(1,128)}, u32[]{:S(2)}) copy-start(f32[1,1536]{1,0:T(1,128)} %param.11) | copy-start | bytes 18436
  57.2 49.5 %copy-start.1 = (bf16[1,40,1536]{2,1,0:T(8,128)(2,1)S(1)}, bf16[1,40,1536]{2,1,0:T(8,128)(2,1)}, u32[]{:S(2)}) copy-start(bf16[1,40,1536]{2,1,0:T(8,128)(2,1)} %param.9) | copy-start | bytes 368644
  57.2 49.5 %copy-start.3 = (f32[1,40]{1,0:T(1,128)S(1)}, f32[1,40]{1,0:T(1,128)}, u32[]{:S(2)}) copy-start(f32[1,40]{1,0:T(1,128)} %param.10) | copy-start | bytes 484
  57.2 25.2 %all-to-all-start.2 = ((bf16[8,40,512]{2,1,0:T(8,128)(2,1)}), bf16[8,40,512]{2,1,0:T(8,128)(2,1)S(1)}, u32[]{:S(2)}, u32[]{:S(2)}) async-start(bf16[8,40,512]{2,1,0:T(8,128)(2,1)} %bitcast.10), calls=%async_computation.3 | async-start | bytes 655360 | tf_op jit(solution)/shard_map/all_to_all | solution.py:11
  95.6 11.1 %all-to-all-start = ((bf16[4,40,1024]{2,1,0:T(8,128)(2,1)}), bf16[4,40,1024]{2,1,0:T(8,128)(2,1)S(1)}, u32[]{:S(2)}, u32[]{:S(2)}) async-start(bf16[4,40,1024]{2,1,0:T(8,128)(2,1)} %bitcast.25), calls=%async_computation.1 | async-start | bytes 655360 | tf_op jit(solution)/shard_map/all_to_all | solution.py:11
Sparse Core Ops, SparseCore 0:
  40.8 54.7 reduce-scatter.1

commit v3 on v2

v3 whole, which is shorter than its diff:
```python
import jax
import jax.numpy as jnp
from jax import lax
from jax.sharding import Mesh, PartitionSpec as P

NX, NZ, NY = 4, 8, 8
PAIR = 2


def local(v_pppp, lam, v_hhpp, hole_energy, part_energy, pp_dim, hh_dim):
    pp_used = pp_dim[0]
    hh_used = hh_dim[0]
    hole_local = lam.shape[1]
    part_local = lam.shape[2]
    y = lax.axis_index("row")
    col = lax.axis_index(("x", "zh", "zl"))
    hole_ids = y * hole_local + jnp.arange(hole_local, dtype=jnp.int32)
    part_ids = col * part_local + jnp.arange(part_local, dtype=jnp.int32)
    keep = (hole_ids[:, None] < hh_used) & (part_ids[None, :] < pp_used)
    masked = jnp.where(keep, lam[0], jnp.zeros_like(lam[0]))
    out_rows = v_hhpp.shape[1]
    out_cols = v_hhpp.shape[2]
    left = lax.all_gather(masked, "row", axis=0, tiled=True)

    by_owner = left.reshape(NX, NZ // PAIR, PAIR, out_rows, part_local).transpose(0, 2, 1, 3, 4)
    part = jnp.dot(by_owner.reshape(NX * NZ * out_rows, part_local), v_pppp[0], preferred_element_type=jnp.float32)
    part = part.astype(jnp.bfloat16).reshape(NX * PAIR, NZ // PAIR * out_rows, out_cols)
    got = lax.all_to_all(part, ("x", "zl"), 0, 0)
    some = jnp.sum(got.astype(jnp.float32), axis=0).astype(jnp.bfloat16)
    got = lax.all_to_all(some.reshape(NZ // PAIR, out_rows, out_cols), "zh", 0, 0)
    ladder = jnp.sum(got.astype(jnp.float32), axis=0)

    out_hole = col * out_rows + jnp.arange(out_rows, dtype=jnp.int32)
    out_part = y * out_cols + jnp.arange(out_cols, dtype=jnp.int32)
    valid = (out_hole[:, None] < hh_used) & (out_part[None, :] < pp_used)
    denom = hole_energy[0][:, None] - part_energy[0][None, :]
    value = (v_hhpp[0].astype(jnp.float32) + ladder) / denom
    result = jnp.where(valid, value, jnp.zeros_like(value)).astype(jnp.bfloat16)
    return result[None]


def solution(mesh):
    split = Mesh(mesh.devices.reshape(2, NY, NX, NZ // PAIR, PAIR), ("grp", "row", "x", "zh", "zl"))
    col = ("x", "zh", "zl")
    return jax.shard_map(
        local,
        mesh=split,
        in_specs=(
            P("grp", col, "row"),
            P("grp", "row", col),
            P("grp", col, "row"),
            P("grp", col),
            P("grp", "row"),
            P("grp"),
            P("grp"),
        ),
        out_specs=P("grp", col, "row"),
        check_vma=False,
    )
```

time: 115 us -> 105 us (0.913)
  blocking collectives: 43.3 us -> 73.6 us
  waiting for transfers between devices: 34.9 us -> 10.8 us
  between operations: 14.8 us -> 1.48 us
  starting transfers between devices: 14.4 us -> 9.66 us
  other arithmetic: 2.93 us -> 5.51 us
  matrix products: 3.86 us -> 2.21 us
    all_to_all x1, blocking collectives: 14.7 us -> 45.1 us  [local(): got = lax.all_to_all(part, ('x', 'zl'), 0, 0)]
    reduce_scatter x1 -> x0, waiting for transfers between devices: 13.1 us -> none  [local(): sum_a = lax.psum_scatter(part_a, 'z', scatter_dimension=0, tiled=True)]
    all_to_all x2 -> x1, waiting for transfers between devices: 21.8 us -> 10.8 us  [local(): lax.all_to_all(some.reshape(NZ // PAIR, out_rows, out_cols), 'zh', 0, 0)]
    all_to_all x2 -> x1, starting transfers between devices: 14.4 us -> 9.66 us  [local(): lax.all_to_all(some.reshape(NZ // PAIR, out_rows, out_cols), 'zh', 0, 0)]
    reduce_sum x3 -> x2, other arithmetic: 1.09 us -> 3.67 us  [the longest x1 3.6 us: local(): some = jnp.sum(got.astype(jnp.float32), axis=0).astype(jnp.bfloat16)]
    dot_general x2 -> x1, matrix products: 3.86 us -> 2.21 us  [local(): jnp.dot(by_owner.reshape(NX * NZ * out_rows, part_local), v_pppp[0], pref...]
  transfers between devices with their start and end apart: 3 -> 1, of which waited for: 3 -> 1; matrix products, arithmetic and copies ran while one was open for 2% -> 0% of each run, Pallas kernels for 0% -> 0%
where the time goes in v3:
time: 105 us; the launch traced here: 103 us
  blocking collectives  73.6 us (70%)
  waiting for transfers between devices  10.8 us (10%)
  starting transfers between devices  9.66 us (9%)
  other arithmetic  5.51 us (5%)
  matrix products  2.21 us (2%)
  between operations  1.48 us (1%)
    all_to_all x1, blocking collectives, local(): got = lax.all_to_all(part, ('x', 'zl'), 0, 0)  45.1 us
    all_gather x1, blocking collectives, local(): left = lax.all_gather(masked, 'row', axis=0, tiled=True)  28.5 us
    all_to_all x1, waiting for transfers between devices, local(): lax.all_to_all(some.reshape(NZ // PAIR, out_rows, out_cols), 'zh', 0, 0)  10.8 us
    all_to_all x1, starting transfers between devices, local(): lax.all_to_all(some.reshape(NZ // PAIR, out_rows, out_cols), 'zh', 0, 0)  9.66 us
    reduce_sum x1, other arithmetic, local(): some = jnp.sum(got.astype(jnp.float32), axis=0).astype(jnp.bfloat16)  3.6 us
    dot_general x1, matrix products, local(): jnp.dot(by_owner.reshape(NX * NZ * out_rows, part_local), v_pppp[0], pref...  2.21 us
  transfers between devices with their start and end apart: 1, of which 1 were waited for; matrix products, arithmetic and copies ran while one was open for 0% of the time, Pallas kernels for 0%

profile of v3, /device:TPU:56, one launch (start us, length us, event | category | flops | bytes accessed | tf_op | source)
XLA Modules:
  0.0 103.3 jit_solution(1396111228123114878)
XLA Ops:
  0.0 0.0 copy-start
  1.4 1.0 and_select_fusion
  2.4 28.5 %all_gather.3 = bf16[1280,384]{1,0:T(8,128)(2,1)S(1)} all-gather(bf16[160,384]{1,0:T(8,128)(2,1)S(1)} %and_select_fusion), channel_id=1, replica_groups=mesh['grp'=2,'row'=8,'x'=4,'zh'=4,'zl'=2] {'row'}, dimensions={0}, use_global_device_ids=true | all-gather | bytes 1105920 | tf_op jit(solution)/shard_map/all_gather | solution.py:23
  30.9 0.1 copy.9
  31.0 0.0 copy-done
  31.0 2.2 %convolution_convert_fusion = bf16[1280,1536]{1,0:T(8,128)(2,1)S(1)} fusion(bf16[1280,384]{1,0:T(8,128)(2,1)S(1)} %bitcast.29, bf16[1,384,1536]{2,1,0:T(8,128)(2,1)S(1)} %copy-done), kind=kOutput, calls=%fused_computation | convolution fusion | flops 1511915520 | bytes 6094848 | tf_op jit(solution)/shard_map/dot_general | solution.py:26
  33.3 45.1 %all_to_all.10 = bf16[8,160,1536]{2,1,0:T(8,128)(2,1)} all-to-all(bf16[8,160,1536]{2,1,0:T(8,128)(2,1)S(1)} %bitcast.27), channel_id=1, replica_groups=mesh['grp'=2,'row'=8,'x'=4,'zh'=4,'zl'=2] {'x','zl'}, dimensions={0} | all-to-all | bytes 7864320 | tf_op jit(solution)/shard_map/all_to_all | solution.py:28
  78.3 0.0 copy-start.2
  78.3 0.0 copy-start.1
  78.3 0.0 copy-start.3
  78.4 3.6 %reduce_sum.23 = bf16[160,1536]{1,0:T(8,128)(2,1)} reduce(bf16[8,160,1536]{2,1,0:T(8,128)(2,1)} %all_to_all.10, bf16[]{:T(256)} %constant.32.clone.1), dimensions={0}, to_apply=%region_0.1 | reduce | flops 1720320 | bytes 4423682 | tf_op jit(solution)/shard_map/reduce_sum | solution.py:29
  82.0 9.7 %all-to-all-start.1 = ((bf16[4,40,1536]{2,1,0:T(8,128)(2,1)}), bf16[4,40,1536]{2,1,0:T(8,128)(2,1)S(1)}, u32[]{:S(2)}, u32[]{:S(2)}) async-start(bf16[4,40,1536]{2,1,0:T(8,128)(2,1)} %bitcast.8), calls=%async_computation.1 | async-start | bytes 983040 | tf_op jit(solution)/shard_map/all_to_all | solution.py:30
  91.6 0.0 copy-done.2
  91.7 10.8 %all-to-all-done.1 = bf16[4,40,1536]{2,1,0:T(8,128)(2,1)S(1)} async-done(((bf16[4,40,1536]{2,1,0:T(8,128)(2,1)}), bf16[4,40,1536]{2,1,0:T(8,128)(2,1)S(1)}, u32[]{:S(2)}, u32[]{:S(2)}) %all-to-all-start.1) | async-done | bytes 491552 | tf_op jit(solution)/shard_map/all_to_all | solution.py:30
  102.4 0.1 convert_reduce_fusion
  102.5 0.0 copy-done.1
  102.5 0.0 copy-done.3
  102.5 0.8 fusion.3
  (5 shorter events, 0.1 us)
Async XLA Ops:
  0.0 31.0 %copy-start = (bf16[1,384,1536]{2,1,0:T(8,128)(2,1)S(1)}, bf16[1,384,1536]{2,1,0:T(8,128)(2,1)}, u32[]{:S(2)}) copy-start(bf16[1,384,1536]{2,1,0:T(8,128)(2,1)} %param.7) | copy-start | bytes 3538948
  78.3 13.3 %copy-start.2 = (f32[1,1536]{1,0:T(1,128)S(1)}, f32[1,1536]{1,0:T(1,128)}, u32[]{:S(2)}) copy-start(f32[1,1536]{1,0:T(1,128)} %param.11) | copy-start | bytes 18436
  78.3 24.2 %copy-start.1 = (bf16[1,40,1536]{2,1,0:T(8,128)(2,1)S(1)}, bf16[1,40,1536]{2,1,0:T(8,128)(2,1)}, u32[]{:S(2)}) copy-start(bf16[1,40,1536]{2,1,0:T(8,128)(2,1)} %param.9) | copy-start | bytes 368644
  78.3 24.2 %copy-start.3 = (f32[1,40]{1,0:T(1,128)S(1)}, f32[1,40]{1,0:T(1,128)}, u32[]{:S(2)}) copy-start(f32[1,40]{1,0:T(1,128)} %param.10) | copy-start | bytes 484
  82.0 20.5 %all-to-all-start.1 = ((bf16[4,40,1536]{2,1,0:T(8,128)(2,1)}), bf16[4,40,1536]{2,1,0:T(8,128)(2,1)S(1)}, u32[]{:S(2)}, u32[]{:S(2)}) async-start(bf16[4,40,1536]{2,1,0:T(8,128)(2,1)} %bitcast.8), calls=%async_computation.1 | async-start | bytes 983040 | tf_op jit(solution)/shard_map/all_to_all | solution.py:30

commit v4 on v3

--- a/solution.py
+++ b/solution.py
@@ -20,12 +20,22 @@
     masked = jnp.where(keep, lam[0], jnp.zeros_like(lam[0]))
     out_rows = v_hhpp.shape[1]
     out_cols = v_hhpp.shape[2]
-    left = lax.all_gather(masked, "row", axis=0, tiled=True)
+    swap = [(0, 1), (1, 0)]
+    odd = lax.axis_index("zl") == 1
 
-    by_owner = left.reshape(NX, NZ // PAIR, PAIR, out_rows, part_local).transpose(0, 2, 1, 3, 4)
-    part = jnp.dot(by_owner.reshape(NX * NZ * out_rows, part_local), v_pppp[0], preferred_element_type=jnp.float32)
-    part = part.astype(jnp.bfloat16).reshape(NX * PAIR, NZ // PAIR * out_rows, out_cols)
-    got = lax.all_to_all(part, ("x", "zl"), 0, 0)
+    halves = masked.reshape(hole_local // (PAIR * out_rows), PAIR, out_rows, part_local)
+    half = (hole_local // PAIR, part_local)
+    kept = jnp.where(odd, halves[:, 1], halves[:, 0]).reshape(half)
+    given = jnp.where(odd, halves[:, 0], halves[:, 1]).reshape(half)
+    taken = lax.ppermute(given, "zl", swap)
+    tile, taken = lax.optimization_barrier((v_pppp[0], taken))
+    other_tile = lax.ppermute(tile, "zl", swap)
+    left = lax.all_gather(jnp.concatenate([kept, taken], axis=1), "row", axis=0, tiled=True)
+    part = jnp.dot(left[:, :part_local], tile, preferred_element_type=jnp.float32)
+    part = part + jnp.dot(left[:, part_local:], other_tile, preferred_element_type=jnp.float32)
+
+    part = part.astype(jnp.bfloat16).reshape(NX, NZ // PAIR * out_rows, out_cols)
+    got = lax.all_to_all(part, "x", 0, 0)
     some = jnp.sum(got.astype(jnp.float32), axis=0).astype(jnp.bfloat16)
     got = lax.all_to_all(some.reshape(NZ // PAIR, out_rows, out_cols), "zh", 0, 0)
     ladder = jnp.sum(got.astype(jnp.float32), axis=0)

time: 105 us -> 92.2 us (0.88)
  the two profiles are of different devices: /device:TPU:56 before, /device:TPU:8 now
where the time goes in v4:
time: 92.2 us; the launch traced here: 91.8 us
  blocking collectives  52.1 us (57%)
  starting transfers between devices  17.6 us (19%)
  waiting for transfers between devices  15.1 us (16%)
  other arithmetic  3.15 us (3%)
  matrix products  2.35 us (3%)
  between operations  1.41 us (2%)
    all_gather x1, blocking collectives, local(): lax.all_gather(jnp.concatenate([kept, taken], axis=1), 'row', axis=0, til...  27.5 us
    all_to_all x1, blocking collectives, local(): got = lax.all_to_all(part, 'x', 0, 0)  24.6 us
    all_to_all x1, waiting for transfers between devices, local(): lax.all_to_all(some.reshape(NZ // PAIR, out_rows, out_cols), 'zh', 0, 0)  12.9 us
    all_to_all x1, starting transfers between devices, local(): lax.all_to_all(some.reshape(NZ // PAIR, out_rows, out_cols), 'zh', 0, 0)  9.39 us
    ppermute x1, starting transfers between devices, local(): taken = lax.ppermute(given, 'zl', swap)  4.28 us
    ppermute x1, starting transfers between devices, local(): other_tile = lax.ppermute(tile, 'zl', swap)  3.91 us
    ppermute x1, waiting for transfers between devices, local(): taken = lax.ppermute(given, 'zl', swap)  2.19 us
  transfers between devices with their start and end apart: 3, of which 2 were waited for; matrix products, arithmetic and copies ran while one was open for 0% of the time, Pallas kernels for 0%

profile of v4, /device:TPU:8, one launch (start us, length us, event | category | flops | bytes accessed | tf_op | source)
XLA Modules:
  0.0 91.8 jit_solution(13484197581955256428)
XLA Ops:
  1.3 1.0 %and_select_fusion = bf16[2,2,40,384]{3,2,1,0:T(8,128)(2,1)S(1)} fusion(bf16[2,2,40,384]{3,2,1,0:T(8,128)(2,1)} %bitcast.27, pred[384]{0:T(512)(128)(4,1)S(1)} %add_compare_fusion.1, pred[2,2,40]{2,1,0:T(4,128)(4,1)S(1)} %add_compare_fusion.2), kind=kLoop, calls=%fused_computation.9 | loop fusion | flops 122880 | bytes 246304 | tf_op jit(solution)/shard_map/jit(_where)/select_n | solution.py:20
  2.4 4.3 %collective-permute-start = (bf16[80,384]{1,0:T(8,128)(2,1)S(1)}, bf16[80,384]{1,0:T(8,128)(2,1)S(1)}, u32[]{:S(2)}, u32[]{:S(2)}) collective-permute-start(bf16[80,384]{1,0:T(8,128)(2,1)S(1)} %bitcast.28), channel_id=1, source_target_pairs={{0,1},{1,0},{2,3},{3,2},{4,5},{5,4},{6,7},{7,6},{8,9},{9,8},{10,11... | collective-permute-start | bytes 184328 | tf_op jit(solution)/shard_map/ppermute | solution.py:30
  6.7 2.2 %collective-permute-done = bf16[80,384]{1,0:T(8,128)(2,1)S(1)} collective-permute-done((bf16[80,384]{1,0:T(8,128)(2,1)S(1)}, bf16[80,384]{1,0:T(8,128)(2,1)S(1)}, u32[]{:S(2)}, u32[]{:S(2)}) %collective-permute-start) | collective-permute-done | bytes 61472 | tf_op jit(solution)/shard_map/ppermute | solution.py:30
  8.9 3.9 %collective-permute-start.1 = (bf16[384,1536]{1,0:T(8,128)(2,1)}, bf16[384,1536]{1,0:T(8,128)(2,1)S(1)}, u32[]{:S(2)}, u32[]{:S(2)}) collective-permute-start(bf16[384,1536]{1,0:T(8,128)(2,1)} %bitcast.24), channel_id=1, source_target_pairs={{0,1},{1,0},{2,3},{3,2},{4,5},{5,4},{6,7},{7,6},{8,9},{9,8},{10,11... | collective-permute-start | bytes 3538952 | tf_op jit(solution)/shard_map/ppermute | solution.py:32
  12.8 27.5 %all_gather.3 = bf16[640,768]{1,0:T(8,128)(2,1)S(1)} all-gather(bf16[80,768]{1,0:T(8,128)(2,1)S(1)} %pad_maximum_fusion), channel_id=1, replica_groups=mesh['grp'=2,'row'=8,'x'=4,'zh'=4,'zl'=2] {'row'}, dimensions={0}, use_global_device_ids=true | all-gather | bytes 1105920 | tf_op jit(solution)/shard_map/all_gather | solution.py:33
  40.3 0.0 copy-start
  40.3 0.0 collective-permute-done.1
  40.3 1.2 %fusion = f32[640,1536]{1,0:T(8,128)S(1)} fusion(bf16[384,1536]{1,0:T(8,128)(2,1)S(1)} %collective-permute-done.1, bf16[640,768]{1,0:T(8,128)(2,1)S(1)} %all_gather.3), kind=kOutput, calls=%fused_computation.2 | convolution fusion | flops 754974720 | bytes 5603328 | tf_op jit(solution)/shard_map/dot_general | solution.py:35
  41.5 0.1 copy-done
  41.6 1.2 %add_convert_fusion = bf16[640,1536]{1,0:T(8,128)(2,1)S(1)} fusion(f32[640,1536]{1,0:T(8,128)S(1)} %fusion, bf16[384,1536]{1,0:T(8,128)(2,1)S(1)} %bitcast.25, bf16[640,768]{1,0:T(8,128)(2,1)S(1)} %all_gather.3), kind=kOutput, calls=%fused_computation | convolution fusion | flops 756940800 | bytes 7569408 | tf_op jit(solution)/shard_map/dot_general | solution.py:34
  42.8 24.6 %all_to_all.10 = bf16[4,160,1536]{2,1,0:T(8,128)(2,1)S(1)} all-to-all(bf16[4,160,1536]{2,1,0:T(8,128)(2,1)S(1)} %bitcast.23), channel_id=1, replica_groups=mesh['grp'=2,'row'=8,'x'=4,'zh'=4,'zl'=2] {'x'}, dimensions={0} | all-to-all | bytes 3932160 | tf_op jit(solution)/shard_map/all_to_all | solution.py:38
  67.4 0.0 copy-start.2
  67.4 0.0 copy-start.1
  67.4 0.0 copy-start.3
  67.4 1.2 %reduce_sum.23 = bf16[160,1536]{1,0:T(8,128)(2,1)} reduce(bf16[4,160,1536]{2,1,0:T(8,128)(2,1)S(1)} %all_to_all.10, bf16[]{:T(256)} %constant.37.clone.1), dimensions={0}, to_apply=%region_0.1 | reduce | flops 737280 | bytes 2457602 | tf_op jit(solution)/shard_map/reduce_sum | solution.py:39
  68.6 9.4 %all-to-all-start.1 = ((bf16[4,40,1536]{2,1,0:T(8,128)(2,1)}), bf16[4,40,1536]{2,1,0:T(8,128)(2,1)S(1)}, u32[]{:S(2)}, u32[]{:S(2)}) async-start(bf16[4,40,1536]{2,1,0:T(8,128)(2,1)} %bitcast.7), calls=%async_computation.1 | async-start | bytes 983040 | tf_op jit(solution)/shard_map/all_to_all | solution.py:40
  78.0 0.0 copy-done.2
  78.0 12.9 %all-to-all-done.1 = bf16[4,40,1536]{2,1,0:T(8,128)(2,1)S(1)} async-done(((bf16[4,40,1536]{2,1,0:T(8,128)(2,1)}), bf16[4,40,1536]{2,1,0:T(8,128)(2,1)S(1)}, u32[]{:S(2)}, u32[]{:S(2)}) %all-to-all-start.1) | async-done | bytes 491552 | tf_op jit(solution)/shard_map/all_to_all | solution.py:40
  91.0 0.1 convert_reduce_fusion
  91.0 0.0 copy-done.1
  91.1 0.0 copy-done.3
  91.1 0.8 fusion.5
  (7 shorter events, 0.1 us)
Async XLA Ops:
  2.4 6.5 %collective-permute-start = (bf16[80,384]{1,0:T(8,128)(2,1)S(1)}, bf16[80,384]{1,0:T(8,128)(2,1)S(1)}, u32[]{:S(2)}, u32[]{:S(2)}) collective-permute-start(bf16[80,384]{1,0:T(8,128)(2,1)S(1)} %bitcast.28), channel_id=1, source_target_pairs={{0,1},{1,0},{2,3},{3,2},{4,5},{5,4},{6,7},{7,6},{8,9},{9,8},{10,11... | collective-permute-start | bytes 184328 | tf_op jit(solution)/shard_map/ppermute | solution.py:30
  8.9 31.5 %collective-permute-start.1 = (bf16[384,1536]{1,0:T(8,128)(2,1)}, bf16[384,1536]{1,0:T(8,128)(2,1)S(1)}, u32[]{:S(2)}, u32[]{:S(2)}) collective-permute-start(bf16[384,1536]{1,0:T(8,128)(2,1)} %bitcast.24), channel_id=1, source_target_pairs={{0,1},{1,0},{2,3},{3,2},{4,5},{5,4},{6,7},{7,6},{8,9},{9,8},{10,11... | collective-permute-start | bytes 3538952 | tf_op jit(solution)/shard_map/ppermute | solution.py:32
  40.3 1.3 %copy-start = (bf16[1,384,1536]{2,1,0:T(8,128)(2,1)S(1)}, bf16[1,384,1536]{2,1,0:T(8,128)(2,1)}, u32[]{:S(2)}) copy-start(bf16[1,384,1536]{2,1,0:T(8,128)(2,1)} %param.7) | copy-start | bytes 3538948
  67.4 10.6 %copy-start.2 = (f32[1,1536]{1,0:T(1,128)S(1)}, f32[1,1536]{1,0:T(1,128)}, u32[]{:S(2)}) copy-start(f32[1,1536]{1,0:T(1,128)} %param.11) | copy-start | bytes 18436
  67.4 23.7 %copy-start.1 = (bf16[1,40,1536]{2,1,0:T(8,128)(2,1)S(1)}, bf16[1,40,1536]{2,1,0:T(8,128)(2,1)}, u32[]{:S(2)}) copy-start(bf16[1,40,1536]{2,1,0:T(8,128)(2,1)} %param.9) | copy-start | bytes 368644
  67.4 23.7 %copy-start.3 = (f32[1,40]{1,0:T(1,128)S(1)}, f32[1,40]{1,0:T(1,128)}, u32[]{:S(2)}) copy-start(f32[1,40]{1,0:T(1,128)} %param.10) | copy-start | bytes 484
  68.6 22.4 %all-to-all-start.1 = ((bf16[4,40,1536]{2,1,0:T(8,128)(2,1)}), bf16[4,40,1536]{2,1,0:T(8,128)(2,1)S(1)}, u32[]{:S(2)}, u32[]{:S(2)}) async-start(bf16[4,40,1536]{2,1,0:T(8,128)(2,1)} %bitcast.7), calls=%async_computation.1 | async-start | bytes 983040 | tf_op jit(solution)/shard_map/all_to_all | solution.py:40

commit v5 on v4

v5 whole, which is shorter than its diff:
```python
import jax
import jax.numpy as jnp
from jax import lax
from jax.sharding import Mesh, PartitionSpec as P

NX, NZ, NY = 4, 8, 8
PAIR = 2


def add_up(parts):
    total = parts[0].astype(jnp.float32)
    for i in range(1, parts.shape[0]):
        total = total + parts[i].astype(jnp.float32)
    return total


def local(v_pppp, lam, v_hhpp, hole_energy, part_energy, pp_dim, hh_dim):
    pp_used = pp_dim[0]
    hh_used = hh_dim[0]
    hole_local = lam.shape[1]
    part_local = lam.shape[2]
    y = lax.axis_index("row")
    col = lax.axis_index(("x", "zh", "zl"))
    out_rows = v_hhpp.shape[1]
    out_cols = v_hhpp.shape[2]
    swap = [(0, 1), (1, 0)]
    odd = lax.axis_index("zl") == 1

    halves = lam[0].reshape(hole_local // (PAIR * out_rows), PAIR, out_rows, part_local)
    half = (hole_local // PAIR, part_local)
    kept = jnp.where(odd, halves[:, 1], halves[:, 0]).reshape(half)
    given = jnp.where(odd, halves[:, 0], halves[:, 1]).reshape(half)
    taken = lax.ppermute(given, "zl", swap)
    tile, taken = lax.optimization_barrier((v_pppp[0], taken))
    other_tile = lax.ppermute(tile, "zl", swap)
    place = lax.axis_index("zl")
    blocks = jnp.arange(hole_local // (PAIR * out_rows), dtype=jnp.int32)
    hole_ids = y * hole_local + (blocks[:, None] * PAIR + place) * out_rows + jnp.arange(out_rows, dtype=jnp.int32)
    part_ids = jnp.stack([col, col + 1 - 2 * place])[:, None] * part_local + jnp.arange(part_local, dtype=jnp.int32)
    keep = (hole_ids.reshape(-1, 1) < hh_used) & (part_ids.reshape(1, -1) < pp_used)
    both = jnp.concatenate([kept, taken], axis=1)
    both = jnp.where(keep, both, jnp.zeros_like(both))
    left = lax.all_gather(both, "row", axis=0, tiled=True)
    out_hole = col * out_rows + jnp.arange(out_rows, dtype=jnp.int32)
    out_part = y * out_cols + jnp.arange(out_cols, dtype=jnp.int32)
    ends = (out_hole < hh_used, out_part < pp_used, hole_energy[0], part_energy[0])
    left, ends = lax.optimization_barrier((left, ends))
    row_ok, col_ok, hole, particle = ends
    part = jnp.dot(left[:, :part_local], tile, preferred_element_type=jnp.float32)
    part = part + jnp.dot(left[:, part_local:], other_tile, preferred_element_type=jnp.float32)

    part = part.astype(jnp.bfloat16).reshape(NX, NZ // PAIR * out_rows, out_cols)
    got = lax.all_to_all(part, "x", 0, 0)
    some = add_up(got).astype(jnp.bfloat16)
    got = lax.all_to_all(some.reshape(NZ // PAIR, out_rows, out_cols), "zh", 0, 0)
    ladder = add_up(got)

    valid = row_ok[:, None] & col_ok[None, :]
    denom = hole[:, None] - particle[None, :]
    value = (v_hhpp[0].astype(jnp.float32) + ladder) / denom
    result = jnp.where(valid, value, jnp.zeros_like(value)).astype(jnp.bfloat16)
    return result[None]


def solution(mesh):
    split = Mesh(mesh.devices.reshape(2, NY, NX, NZ // PAIR, PAIR), ("grp", "row", "x", "zh", "zl"))
    col = ("x", "zh", "zl")
    return jax.shard_map(
        local,
        mesh=split,
        in_specs=(
            P("grp", col, "row"),
            P("grp", "row", col),
            P("grp", col, "row"),
            P("grp", col),
            P("grp", "row"),
            P("grp"),
            P("grp"),
        ),
        out_specs=P("grp", col, "row"),
        check_vma=False,
    )
```

time: 92.2 us -> 89.1 us (0.966)
  the two profiles are of different devices: /device:TPU:8 before, /device:TPU:56 now
where the time goes in v5:
time: 89.1 us; the launch traced here: 88.7 us
  blocking collectives  72.9 us (82%)
  starting transfers between devices  8.19 us (9%)
  other arithmetic  3 us (3%)
  matrix products  2.35 us (3%)
  between operations  1.37 us (2%)
    all_gather x1, blocking collectives, local(): left = lax.all_gather(both, 'row', axis=0, tiled=True)  26.8 us
    all_to_all x1, blocking collectives, local(): got = lax.all_to_all(part, 'x', 0, 0)  24.3 us
    all_to_all x1, blocking collectives, local(): lax.all_to_all(some.reshape(NZ // PAIR, out_rows, out_cols), 'zh', 0, 0)  21.8 us
    ppermute x1, starting transfers between devices, local(): taken = lax.ppermute(given, 'zl', swap)  4.28 us
    ppermute x1, starting transfers between devices, local(): other_tile = lax.ppermute(tile, 'zl', swap)  3.91 us
  transfers between devices with their start and end apart: 2, of which 1 were waited for; matrix products, arithmetic and copies ran while one was open for 1% of the time, Pallas kernels for 0%

profile of v5, /device:TPU:56, one launch (start us, length us, event | category | flops | bytes accessed | tf_op | source)
XLA Modules:
  0.0 88.7 jit_solution(12528149745196995245)
XLA Ops:
  0.0 0.9 broadcast_select_fusion.1
  0.9 4.3 %collective-permute-start = (bf16[80,384]{1,0:T(8,128)(2,1)S(1)}, bf16[80,384]{1,0:T(8,128)(2,1)S(1)}, u32[]{:S(2)}, u32[]{:S(2)}) collective-permute-start(bf16[80,384]{1,0:T(8,128)(2,1)S(1)} %bitcast.23), channel_id=1, source_target_pairs={{0,1},{1,0},{2,3},{3,2},{4,5},{5,4},{6,7},{7,6},{8,9},{9,8},{10,11... | collective-permute-start | bytes 184328 | tf_op jit(solution)/shard_map/ppermute | solution.py:33
  5.8 0.1 add_compare_fusion.2
  6.6 0.1 lt.42
  6.6 0.7 collective-permute-done
  7.4 3.9 %collective-permute-start.1 = (bf16[384,1536]{1,0:T(8,128)(2,1)}, bf16[384,1536]{1,0:T(8,128)(2,1)S(1)}, u32[]{:S(2)}, u32[]{:S(2)}) collective-permute-start(bf16[384,1536]{1,0:T(8,128)(2,1)} %bitcast.19), channel_id=1, source_target_pairs={{0,1},{1,0},{2,3},{3,2},{4,5},{5,4},{6,7},{7,6},{8,9},{9,8},{10,11... | collective-permute-start | bytes 3538952 | tf_op jit(solution)/shard_map/ppermute | solution.py:35
  11.3 0.1 add_multiply_fusion
  11.4 0.1 add_compare_fusion.1
  11.4 0.7 reduce
  12.2 0.1 and_select_fusion
  12.3 26.8 %all_gather.3 = bf16[640,768]{1,0:T(8,128)(2,1)S(1)} all-gather(bf16[80,768]{1,0:T(8,128)(2,1)S(1)} %and_select_fusion), channel_id=1, replica_groups=mesh['grp'=2,'row'=8,'x'=4,'zh'=4,'zl'=2] {'row'}, dimensions={0}, use_global_device_ids=true | all-gather | bytes 1105920 | tf_op jit(solution)/shard_map/all_gather | solution.py:43
  39.2 0.0 copy-start
  39.2 0.0 collective-permute-done.1
  39.2 1.2 %fusion = f32[640,1536]{1,0:T(8,128)S(1)} fusion(bf16[384,1536]{1,0:T(8,128)(2,1)S(1)} %collective-permute-done.1, bf16[640,768]{1,0:T(8,128)(2,1)S(1)} %all_gather.3), kind=kOutput, calls=%fused_computation.2 | convolution fusion | flops 754974720 | bytes 5603328 | tf_op jit(solution)/shard_map/dot_general | solution.py:50
  40.3 0.1 copy-done
  40.4 1.2 %add_convert_fusion = bf16[640,1536]{1,0:T(8,128)(2,1)S(1)} fusion(f32[640,1536]{1,0:T(8,128)S(1)} %fusion, bf16[384,1536]{1,0:T(8,128)(2,1)S(1)} %bitcast.20, bf16[640,768]{1,0:T(8,128)(2,1)S(1)} %all_gather.3), kind=kOutput, calls=%fused_computation | convolution fusion | flops 756940800 | bytes 7569408 | tf_op jit(solution)/shard_map/dot_general | solution.py:49
  41.6 24.3 %all_to_all.10 = bf16[4,160,1536]{2,1,0:T(8,128)(2,1)S(1)} all-to-all(bf16[4,160,1536]{2,1,0:T(8,128)(2,1)S(1)} %bitcast.17), channel_id=1, replica_groups=mesh['grp'=2,'row'=8,'x'=4,'zh'=4,'zl'=2] {'x'}, dimensions={0} | all-to-all | bytes 3932160 | tf_op jit(solution)/shard_map/all_to_all | solution.py:53
  65.9 0.0 copy-start.1
  65.9 0.0 copy-start.2
  65.9 0.2 add_convert_fusion.1
  66.1 21.8 %all_to_all.11 = bf16[4,40,1536]{2,1,0:T(8,128)(2,1)S(1)} all-to-all(bf16[4,40,1536]{2,1,0:T(8,128)(2,1)S(1)} %bitcast.18), channel_id=1, replica_groups=mesh['grp'=2,'row'=8,'x'=4,'zh'=4,'zl'=2] {'zh'}, dimensions={0} | all-to-all | bytes 983040 | tf_op jit(solution)/shard_map/all_to_all | solution.py:55
  87.9 0.0 copy-done.1
  87.9 0.0 copy-done.2
  87.9 0.8 select_convert_fusion
  (4 shorter events, 0.0 us)
Async XLA Ops:
  0.9 6.5 %collective-permute-start = (bf16[80,384]{1,0:T(8,128)(2,1)S(1)}, bf16[80,384]{1,0:T(8,128)(2,1)S(1)}, u32[]{:S(2)}, u32[]{:S(2)}) collective-permute-start(bf16[80,384]{1,0:T(8,128)(2,1)S(1)} %bitcast.23), channel_id=1, source_target_pairs={{0,1},{1,0},{2,3},{3,2},{4,5},{5,4},{6,7},{7,6},{8,9},{9,8},{10,11... | collective-permute-start | bytes 184328 | tf_op jit(solution)/shard_map/ppermute | solution.py:33
  7.4 31.8 %collective-permute-start.1 = (bf16[384,1536]{1,0:T(8,128)(2,1)}, bf16[384,1536]{1,0:T(8,128)(2,1)S(1)}, u32[]{:S(2)}, u32[]{:S(2)}) collective-permute-start(bf16[384,1536]{1,0:T(8,128)(2,1)} %bitcast.19), channel_id=1, source_target_pairs={{0,1},{1,0},{2,3},{3,2},{4,5},{5,4},{6,7},{7,6},{8,9},{9,8},{10,11... | collective-permute-start | bytes 3538952 | tf_op jit(solution)/shard_map/ppermute | solution.py:35
  39.2 1.3 %copy-start = (bf16[1,384,1536]{2,1,0:T(8,128)(2,1)S(1)}, bf16[1,384,1536]{2,1,0:T(8,128)(2,1)}, u32[]{:S(2)}) copy-start(bf16[1,384,1536]{2,1,0:T(8,128)(2,1)} %param.7) | copy-start | bytes 3538948
  65.9 22.0 %copy-start.1 = (bf16[1,40,1536]{2,1,0:T(8,128)(2,1)S(1)}, bf16[1,40,1536]{2,1,0:T(8,128)(2,1)}, u32[]{:S(2)}) copy-start(bf16[1,40,1536]{2,1,0:T(8,128)(2,1)} %param.9) | copy-start | bytes 368644
  65.9 22.0 %copy-start.2 = (f32[1,40]{1,0:T(1,128)S(1)}, f32[1,40]{1,0:T(1,128)}, u32[]{:S(2)}) copy-start(f32[1,40]{1,0:T(1,128)} %param.10) | copy-start | bytes 484

commit v6 on v5

--- a/solution.py
+++ b/solution.py
@@ -24,16 +24,15 @@
     out_rows = v_hhpp.shape[1]
     out_cols = v_hhpp.shape[2]
     swap = [(0, 1), (1, 0)]
-    odd = lax.axis_index("zl") == 1
 
     halves = lam[0].reshape(hole_local // (PAIR * out_rows), PAIR, out_rows, part_local)
     half = (hole_local // PAIR, part_local)
-    kept = jnp.where(odd, halves[:, 1], halves[:, 0]).reshape(half)
-    given = jnp.where(odd, halves[:, 0], halves[:, 1]).reshape(half)
-    taken = lax.ppermute(given, "zl", swap)
-    tile, taken = lax.optimization_barrier((v_pppp[0], taken))
+    place = lax.axis_index("zl")
+    kept = lax.dynamic_slice_in_dim(halves, place, 1, 1).reshape(half)
+    pair = lax.all_gather(halves, "zl")
+    tile, pair = lax.optimization_barrier((v_pppp[0], pair))
+    taken = lax.dynamic_slice(pair, (1 - place, 0, place, 0, 0), (1, hole_local // (PAIR * out_rows), 1, out_rows, part_local)).reshape(half)
     other_tile = lax.ppermute(tile, "zl", swap)
-    place = lax.axis_index("zl")
     blocks = jnp.arange(hole_local // (PAIR * out_rows), dtype=jnp.int32)
     hole_ids = y * hole_local + (blocks[:, None] * PAIR + place) * out_rows + jnp.arange(out_rows, dtype=jnp.int32)
     part_ids = jnp.stack([col, col + 1 - 2 * place])[:, None] * part_local + jnp.arange(part_local, dtype=jnp.int32)
@@ -43,7 +42,7 @@
     left = lax.all_gather(both, "row", axis=0, tiled=True)
     out_hole = col * out_rows + jnp.arange(out_rows, dtype=jnp.int32)
     out_part = y * out_cols + jnp.arange(out_cols, dtype=jnp.int32)
-    ends = (out_hole < hh_used, out_part < pp_used, hole_energy[0], part_energy[0])
+    ends = (out_hole < hh_used, out_part < pp_used, hole_energy[0], part_energy)
     left, ends = lax.optimization_barrier((left, ends))
     row_ok, col_ok, hole, particle = ends
     part = jnp.dot(left[:, :part_local], tile, preferred_element_type=jnp.float32)
@@ -56,7 +55,7 @@
     ladder = add_up(got)
 
     valid = row_ok[:, None] & col_ok[None, :]
-    denom = hole[:, None] - particle[None, :]
+    denom = hole[:, None] - particle
     value = (v_hhpp[0].astype(jnp.float32) + ladder) / denom
     result = jnp.where(valid, value, jnp.zeros_like(value)).astype(jnp.bfloat16)
     return result[None]

time: 89.1 us -> 88.3 us (level)
  blocking collectives: 72.9 us -> 56.2 us
  waiting for transfers between devices: 0.71 us -> 11.1 us
  starting transfers between devices: 8.19 us -> 13 us
    all_to_all x1 -> x0, blocking collectives: 21.8 us -> none  [local(): lax.all_to_all(some.reshape(NZ // PAIR, out_rows, out_cols), 'zh', 0, 0)]
    all_to_all x0 -> x1, waiting for transfers between devices: none -> 11.1 us  [local(): lax.all_to_all(some.reshape(NZ // PAIR, out_rows, out_cols), 'zh', 0, 0)]
    all_to_all x0 -> x1, starting transfers between devices: none -> 9.4 us  [local(): lax.all_to_all(some.reshape(NZ // PAIR, out_rows, out_cols), 'zh', 0, 0)]
    all_gather x0 -> x1, blocking collectives: none -> 6.74 us  [local(): pair = lax.all_gather(halves, 'zl')]
    ppermute x1 -> x0, starting transfers between devices: 4.28 us -> none  [local(): taken = lax.ppermute(given, 'zl', swap)]
    all_to_all x1, blocking collectives: 24.3 us -> 22.3 us  [local(): got = lax.all_to_all(part, 'x', 0, 0)]
  transfers between devices with their start and end apart: 2 -> 2, of which waited for: 1 -> 1; matrix products, arithmetic and copies ran while one was open for 1% -> 3% of each run, Pallas kernels for 0% -> 0%
where the time goes in v6:
time: 88.3 us; the launch traced here: 87.3 us
  blocking collectives  56.2 us (64%)
  starting transfers between devices  13 us (15%)
  waiting for transfers between devices  11.1 us (13%)
  matrix products  2.35 us (3%)
  other arithmetic  2.21 us (3%)
  between operations  1.38 us (2%)
  local copies, waits for them, and re-layouts  0.96 us (1%)
    all_gather x1, blocking collectives, local(): left = lax.all_gather(both, 'row', axis=0, tiled=True)  27.2 us
    all_to_all x1, blocking collectives, local(): got = lax.all_to_all(part, 'x', 0, 0)  22.3 us
    all_to_all x1, waiting for transfers between devices, local(): lax.all_to_all(some.reshape(NZ // PAIR, out_rows, out_cols), 'zh', 0, 0)  11.1 us
    all_to_all x1, starting transfers between devices, local(): lax.all_to_all(some.reshape(NZ // PAIR, out_rows, out_cols), 'zh', 0, 0)  9.4 us
    all_gather x1, blocking collectives, local(): pair = lax.all_gather(halves, 'zl')  6.74 us
    ppermute x1, starting transfers between devices, local(): other_tile = lax.ppermute(tile, 'zl', swap)  3.6 us
  transfers between devices with their start and end apart: 2, of which 1 were waited for; matrix products, arithmetic and copies ran while one was open for 3% of the time, Pallas kernels for 0%

profile of v6, /device:TPU:56, one launch (start us, length us, event | category | flops | bytes accessed | tf_op | source)
XLA Modules:
  0.0 87.3 jit_solution(6421339358352808967)
XLA Ops:
  0.0 0.0 copy-start
  0.0 6.7 %all_gather.6 = bf16[2,2,2,40,384]{4,3,2,1,0:T(8,128)(2,1)S(1)} all-gather(bf16[1,2,2,40,384]{4,3,2,1,0:T(8,128)(2,1)} %bitcast.21), channel_id=1, replica_groups=mesh['grp'=2,'row'=8,'x'=4,'zh'=4,'zl'=2] {'zl'}, dimensions={0}, use_global_device_ids=true | all-gather | bytes 368640 | tf_op jit(solution)/shard_map/all_gather | solution.py:32
  6.7 3.6 %collective-permute-start = (bf16[384,1536]{1,0:T(8,128)(2,1)}, bf16[384,1536]{1,0:T(8,128)(2,1)S(1)}, u32[]{:S(2)}, u32[]{:S(2)}) collective-permute-start(bf16[384,1536]{1,0:T(8,128)(2,1)} %bitcast.19), channel_id=1, source_target_pairs={{0,1},{1,0},{2,3},{3,2},{4,5},{5,4},{6,7},{7,6},{8,9},{9,8},{10,11... | collective-permute-start | bytes 3538952 | tf_op jit(solution)/shard_map/ppermute | solution.py:35
  11.7 0.1 add_multiply_fusion
  11.8 0.1 add_compare_fusion.1
  11.8 0.8 constant_dynamic-slice_fusion.1
  12.7 0.1 add_compare_fusion.2
  12.8 0.1 lt.49
  12.9 0.1 and_select_fusion
  13.0 27.2 %all_gather.7 = bf16[640,768]{1,0:T(8,128)(2,1)S(1)} all-gather(bf16[80,768]{1,0:T(8,128)(2,1)S(1)} %and_select_fusion), channel_id=1, replica_groups=mesh['grp'=2,'row'=8,'x'=4,'zh'=4,'zl'=2] {'row'}, dimensions={0}, use_global_device_ids=true | all-gather | bytes 1105920 | tf_op jit(solution)/shard_map/all_gather | solution.py:42
  40.2 0.0 copy-done
  40.2 1.2 %fusion.1 = f32[640,1536]{1,0:T(8,128)S(1)} fusion(bf16[384,1536]{1,0:T(8,128)(2,1)S(1)} %bitcast.20, bf16[640,768]{1,0:T(8,128)(2,1)S(1)} %all_gather.7), kind=kOutput, calls=%fused_computation.3 | convolution fusion | flops 754974720 | bytes 5603328 | tf_op jit(solution)/shard_map/dot_general | solution.py:48
  41.4 0.0 collective-permute-done
  41.4 1.2 %add_convert_fusion = bf16[640,1536]{1,0:T(8,128)(2,1)S(1)} fusion(f32[640,1536]{1,0:T(8,128)S(1)} %fusion.1, bf16[384,1536]{1,0:T(8,128)(2,1)S(1)} %collective-permute-done, bf16[640,768]{1,0:T(8,128)(2,1)S(1)} %all_gather.7), kind=kOutput, calls=%fused_computation | convolution fusion | flops 756940800 | bytes 7569408 | tf_op jit(solution)/shard_map/dot_general | solution.py:49
  42.6 22.3 %all_to_all.10 = bf16[4,160,1536]{2,1,0:T(8,128)(2,1)S(1)} all-to-all(bf16[4,160,1536]{2,1,0:T(8,128)(2,1)S(1)} %bitcast.18), channel_id=1, replica_groups=mesh['grp'=2,'row'=8,'x'=4,'zh'=4,'zl'=2] {'x'}, dimensions={0} | all-to-all | bytes 3932160 | tf_op jit(solution)/shard_map/all_to_all | solution.py:52
  64.9 0.0 copy-start.2
  64.9 0.0 copy-start.1
  64.9 0.0 copy-start.3
  64.9 1.0 %add_convert_fusion.1 = bf16[1,160,1536]{2,1,0:T(8,128)(2,1)} fusion(bf16[4,160,1536]{2,1,0:T(8,128)(2,1)S(1)} %all_to_all.10), kind=kLoop, calls=%fused_computation.1 | loop fusion | flops 1966080 | bytes 2457600 | tf_op jit(solution)/shard_map/convert
  65.9 9.4 %all-to-all-start.1 = ((bf16[4,40,1536]{2,1,0:T(8,128)(2,1)}), bf16[4,40,1536]{2,1,0:T(8,128)(2,1)S(1)}, u32[]{:S(2)}, u32[]{:S(2)}) async-start(bf16[4,40,1536]{2,1,0:T(8,128)(2,1)} %bitcast.11), calls=%async_computation.1 | async-start | bytes 983040 | tf_op jit(solution)/shard_map/all_to_all | solution.py:54
  75.3 0.0 copy-done.2
  75.3 11.1 %all-to-all-done.1 = bf16[4,40,1536]{2,1,0:T(8,128)(2,1)S(1)} async-done(((bf16[4,40,1536]{2,1,0:T(8,128)(2,1)}), bf16[4,40,1536]{2,1,0:T(8,128)(2,1)S(1)}, u32[]{:S(2)}, u32[]{:S(2)}) %all-to-all-start.1) | async-done | bytes 491552 | tf_op jit(solution)/shard_map/all_to_all | solution.py:54
  86.5 0.0 copy-done.1
  86.5 0.0 copy-done.3
  86.5 0.8 select_convert_fusion
  (6 shorter events, 0.1 us)
Async XLA Ops:
  0.0 40.2 %copy-start = (bf16[1,384,1536]{2,1,0:T(8,128)(2,1)S(1)}, bf16[1,384,1536]{2,1,0:T(8,128)(2,1)}, u32[]{:S(2)}) copy-start(bf16[1,384,1536]{2,1,0:T(8,128)(2,1)} %param.7) | copy-start | bytes 3538948
  6.7 34.6 %collective-permute-start = (bf16[384,1536]{1,0:T(8,128)(2,1)}, bf16[384,1536]{1,0:T(8,128)(2,1)S(1)}, u32[]{:S(2)}, u32[]{:S(2)}) collective-permute-start(bf16[384,1536]{1,0:T(8,128)(2,1)} %bitcast.19), channel_id=1, source_target_pairs={{0,1},{1,0},{2,3},{3,2},{4,5},{5,4},{6,7},{7,6},{8,9},{9,8},{10,11... | collective-permute-start | bytes 3538952 | tf_op jit(solution)/shard_map/ppermute | solution.py:35
  64.9 10.4 %copy-start.2 = (f32[1,1536]{1,0:T(1,128)S(1)}, f32[1,1536]{1,0:T(1,128)}, u32[]{:S(2)}) copy-start(f32[1,1536]{1,0:T(1,128)} %param.11) | copy-start | bytes 18436
  64.9 21.6 %copy-start.1 = (bf16[1,40,1536]{2,1,0:T(8,128)(2,1)S(1)}, bf16[1,40,1536]{2,1,0:T(8,128)(2,1)}, u32[]{:S(2)}) copy-start(bf16[1,40,1536]{2,1,0:T(8,128)(2,1)} %param.9) | copy-start | bytes 368644
  64.9 21.6 %copy-start.3 = (f32[1,40]{1,0:T(1,128)S(1)}, f32[1,40]{1,0:T(1,128)}, u32[]{:S(2)}) copy-start(f32[1,40]{1,0:T(1,128)} %param.10) | copy-start | bytes 484
  65.9 20.6 %all-to-all-start.1 = ((bf16[4,40,1536]{2,1,0:T(8,128)(2,1)}), bf16[4,40,1536]{2,1,0:T(8,128)(2,1)S(1)}, u32[]{:S(2)}, u32[]{:S(2)}) async-start(bf16[4,40,1536]{2,1,0:T(8,128)(2,1)} %bitcast.11), calls=%async_computation.1 | async-start | bytes 983040 | tf_op jit(solution)/shard_map/all_to_all | solution.py:54

commit v7 on v6

--- a/solution.py
+++ b/solution.py
@@ -29,9 +29,11 @@
     half = (hole_local // PAIR, part_local)
     place = lax.axis_index("zl")
     kept = lax.dynamic_slice_in_dim(halves, place, 1, 1).reshape(half)
-    pair = lax.all_gather(halves, "zl")
+    given = lax.dynamic_slice_in_dim(halves, 1 - place, 1, 1).reshape(half)
+    kept, given = lax.optimization_barrier((kept, given))
+    pair = lax.all_gather(given, "zl")
     tile, pair = lax.optimization_barrier((v_pppp[0], pair))
-    taken = lax.dynamic_slice(pair, (1 - place, 0, place, 0, 0), (1, hole_local // (PAIR * out_rows), 1, out_rows, part_local)).reshape(half)
+    taken = jnp.where(place == 1, pair[0], pair[1])
     other_tile = lax.ppermute(tile, "zl", swap)
     blocks = jnp.arange(hole_local // (PAIR * out_rows), dtype=jnp.int32)
     hole_ids = y * hole_local + (blocks[:, None] * PAIR + place) * out_rows + jnp.arange(out_rows, dtype=jnp.int32)
@@ -40,11 +42,6 @@
     both = jnp.concatenate([kept, taken], axis=1)
     both = jnp.where(keep, both, jnp.zeros_like(both))
     left = lax.all_gather(both, "row", axis=0, tiled=True)
-    out_hole = col * out_rows + jnp.arange(out_rows, dtype=jnp.int32)
-    out_part = y * out_cols + jnp.arange(out_cols, dtype=jnp.int32)
-    ends = (out_hole < hh_used, out_part < pp_used, hole_energy[0], part_energy)
-    left, ends = lax.optimization_barrier((left, ends))
-    row_ok, col_ok, hole, particle = ends
     part = jnp.dot(left[:, :part_local], tile, preferred_element_type=jnp.float32)
     part = part + jnp.dot(left[:, part_local:], other_tile, preferred_element_type=jnp.float32)
 
@@ -54,6 +51,10 @@
     got = lax.all_to_all(some.reshape(NZ // PAIR, out_rows, out_cols), "zh", 0, 0)
     ladder = add_up(got)
 
+    out_hole = col * out_rows + jnp.arange(out_rows, dtype=jnp.int32)
+    out_part = y * out_cols + jnp.arange(out_cols, dtype=jnp.int32)
+    row_ok, col_ok = out_hole < hh_used, out_part < pp_used
+    hole, particle = hole_energy[0], part_energy[0][None, :]
     valid = row_ok[:, None] & col_ok[None, :]
     denom = hole[:, None] - particle
     value = (v_hhpp[0].astype(jnp.float32) + ladder) / denom

time: 88.3 us -> 86.8 us (0.983)
  blocking collectives: 56.2 us -> 54.6 us
    all_gather x1, blocking collectives: 6.74 us -> 5.23 us  [local(): pair = lax.all_gather(given, 'zl')]
  transfers between devices with their start and end apart: 2 -> 2, of which waited for: 1 -> 1; matrix products, arithmetic and copies ran while one was open for 3% -> 2% of each run, Pallas kernels for 0% -> 0%
where the time goes in v7:
time: 86.8 us; the launch traced here: 86.4 us
  blocking collectives  54.6 us (63%)
  starting transfers between devices  13.3 us (15%)
  waiting for transfers between devices  11.5 us (13%)
  matrix products  2.35 us (3%)
  other arithmetic  2.23 us (3%)
  between operations  1.38 us (2%)
  local copies, waits for them, and re-layouts  1.09 us (1%)
    all_gather x1, blocking collectives, local(): left = lax.all_gather(both, 'row', axis=0, tiled=True)  26.8 us
    all_to_all x1, blocking collectives, local(): got = lax.all_to_all(part, 'x', 0, 0)  22.5 us
    all_to_all x1, waiting for transfers between devices, local(): lax.all_to_all(some.reshape(NZ // PAIR, out_rows, out_cols), 'zh', 0, 0)  11.5 us
    all_to_all x1, starting transfers between devices, local(): lax.all_to_all(some.reshape(NZ // PAIR, out_rows, out_cols), 'zh', 0, 0)  9.4 us
    all_gather x1, blocking collectives, local(): pair = lax.all_gather(given, 'zl')  5.23 us
    ppermute x1, starting transfers between devices, local(): other_tile = lax.ppermute(tile, 'zl', swap)  3.94 us
  transfers between devices with their start and end apart: 2, of which 1 were waited for; matrix products, arithmetic and copies ran while one was open for 2% of the time, Pallas kernels for 0%

profile of v7, /device:TPU:56, one launch (start us, length us, event | category | flops | bytes accessed | tf_op | source)
XLA Modules:
  0.0 86.4 jit_solution(524073006985035531)
XLA Ops:
  0.0 0.0 copy-start
  0.0 1.0 %constant_dynamic-slice_fusion = (bf16[2,1,40,384]{3,2,1,0:T(8,128)(2,1)S(1)}, bf16[2,1,40,384]{3,2,1,0:T(8,128)(2,1)S(1)}) fusion(bf16[2,2,40,384]{3,2,1,0:T(8,128)(2,1)} %bitcast.26, s32[]{:T(128)S(6)} %select_n.27, s32[]{:T(128)S(6)} %select_n.26), kind=kLoop, calls=%fused_computation.12 | loop fusion | bytes 245768 | tf_op jit(solution)/shard_map/dynamic_slice | solution.py:32
  1.0 5.2 %all-gather = bf16[160,384]{1,0:T(8,128)(2,1)S(1)} all-gather(bf16[80,384]{1,0:T(8,128)(2,1)S(1)} %bitcast.24), channel_id=2, replica_groups=mesh['grp'=2,'row'=8,'x'=4,'zh'=4,'zl'=2] {'zl'}, dimensions={0}, use_global_device_ids=true | all-gather | bytes 184320 | tf_op jit(solution)/shard_map/all_gather | solution.py:34
  6.2 3.9 %collective-permute-start = (bf16[384,1536]{1,0:T(8,128)(2,1)}, bf16[384,1536]{1,0:T(8,128)(2,1)S(1)}, u32[]{:S(2)}, u32[]{:S(2)}) collective-permute-start(bf16[384,1536]{1,0:T(8,128)(2,1)} %bitcast.21), channel_id=1, source_target_pairs={{0,1},{1,0},{2,3},{3,2},{4,5},{5,4},{6,7},{7,6},{8,9},{9,8},{10,11... | collective-permute-start | bytes 3538952 | tf_op jit(solution)/shard_map/ppermute | solution.py:37
  10.8 0.1 add_multiply_fusion
  10.9 0.1 add_compare_fusion.1
  11.6 0.1 add_compare_fusion.2
  11.7 0.1 lt.60
  11.8 0.1 and_select_fusion
  11.9 26.8 %all_gather.11 = bf16[640,768]{1,0:T(8,128)(2,1)S(1)} all-gather(bf16[80,768]{1,0:T(8,128)(2,1)S(1)} %and_select_fusion), channel_id=1, replica_groups=mesh['grp'=2,'row'=8,'x'=4,'zh'=4,'zl'=2] {'row'}, dimensions={0}, use_global_device_ids=true | all-gather | bytes 1105920 | tf_op jit(solution)/shard_map/all_gather | solution.py:44
  38.8 0.0 copy-done
  38.8 1.2 %fusion.1 = f32[640,1536]{1,0:T(8,128)S(1)} fusion(bf16[384,1536]{1,0:T(8,128)(2,1)S(1)} %bitcast.22, bf16[640,768]{1,0:T(8,128)(2,1)S(1)} %all_gather.11), kind=kOutput, calls=%fused_computation.3 | convolution fusion | flops 754974720 | bytes 5603328 | tf_op jit(solution)/shard_map/dot_general | solution.py:45
  40.0 0.0 collective-permute-done
  40.0 1.2 %add_convert_fusion = bf16[640,1536]{1,0:T(8,128)(2,1)S(1)} fusion(f32[640,1536]{1,0:T(8,128)S(1)} %fusion.1, bf16[384,1536]{1,0:T(8,128)(2,1)S(1)} %collective-permute-done, bf16[640,768]{1,0:T(8,128)(2,1)S(1)} %all_gather.11), kind=kOutput, calls=%fused_computation | convolution fusion | flops 756940800 | bytes 7569408 | tf_op jit(solution)/shard_map/dot_general | solution.py:46
  41.2 22.5 %all_to_all.10 = bf16[4,160,1536]{2,1,0:T(8,128)(2,1)S(1)} all-to-all(bf16[4,160,1536]{2,1,0:T(8,128)(2,1)S(1)} %bitcast.20), channel_id=1, replica_groups=mesh['grp'=2,'row'=8,'x'=4,'zh'=4,'zl'=2] {'x'}, dimensions={0} | all-to-all | bytes 3932160 | tf_op jit(solution)/shard_map/all_to_all | solution.py:49
  63.7 0.0 copy-start.2
  63.7 0.0 copy-start.1
  63.7 0.0 copy-start.3
  63.7 1.0 %add_convert_fusion.1 = bf16[1,160,1536]{2,1,0:T(8,128)(2,1)} fusion(bf16[4,160,1536]{2,1,0:T(8,128)(2,1)S(1)} %all_to_all.10), kind=kLoop, calls=%fused_computation.1 | loop fusion | flops 1966080 | bytes 2457600 | tf_op jit(solution)/shard_map/convert
  64.7 9.4 %all-to-all-start.1 = ((bf16[4,40,1536]{2,1,0:T(8,128)(2,1)}), bf16[4,40,1536]{2,1,0:T(8,128)(2,1)S(1)}, u32[]{:S(2)}, u32[]{:S(2)}) async-start(bf16[4,40,1536]{2,1,0:T(8,128)(2,1)} %bitcast.11), calls=%async_computation.1 | async-start | bytes 983040 | tf_op jit(solution)/shard_map/all_to_all | solution.py:51
  74.1 0.0 copy-done.2
  74.2 11.5 %all-to-all-done.1 = bf16[4,40,1536]{2,1,0:T(8,128)(2,1)S(1)} async-done(((bf16[4,40,1536]{2,1,0:T(8,128)(2,1)}), bf16[4,40,1536]{2,1,0:T(8,128)(2,1)S(1)}, u32[]{:S(2)}, u32[]{:S(2)}) %all-to-all-start.1) | async-done | bytes 491552 | tf_op jit(solution)/shard_map/all_to_all | solution.py:51
  85.6 0.0 copy-done.1
  85.6 0.0 copy-done.3
  85.6 0.8 select_convert_fusion
  (6 shorter events, 0.1 us)
Async XLA Ops:
  0.0 38.8 %copy-start = (bf16[1,384,1536]{2,1,0:T(8,128)(2,1)S(1)}, bf16[1,384,1536]{2,1,0:T(8,128)(2,1)}, u32[]{:S(2)}) copy-start(bf16[1,384,1536]{2,1,0:T(8,128)(2,1)} %param.7) | copy-start | bytes 3538948
  6.2 33.8 %collective-permute-start = (bf16[384,1536]{1,0:T(8,128)(2,1)}, bf16[384,1536]{1,0:T(8,128)(2,1)S(1)}, u32[]{:S(2)}, u32[]{:S(2)}) collective-permute-start(bf16[384,1536]{1,0:T(8,128)(2,1)} %bitcast.21), channel_id=1, source_target_pairs={{0,1},{1,0},{2,3},{3,2},{4,5},{5,4},{6,7},{7,6},{8,9},{9,8},{10,11... | collective-permute-start | bytes 3538952 | tf_op jit(solution)/shard_map/ppermute | solution.py:37
  63.7 10.4 %copy-start.2 = (f32[1,1536]{1,0:T(1,128)S(1)}, f32[1,1536]{1,0:T(1,128)}, u32[]{:S(2)}) copy-start(f32[1,1536]{1,0:T(1,128)} %param.11) | copy-start | bytes 18436
  63.7 21.9 %copy-start.1 = (bf16[1,40,1536]{2,1,0:T(8,128)(2,1)S(1)}, bf16[1,40,1536]{2,1,0:T(8,128)(2,1)}, u32[]{:S(2)}) copy-start(bf16[1,40,1536]{2,1,0:T(8,128)(2,1)} %param.9) | copy-start | bytes 368644
  63.7 21.9 %copy-start.3 = (f32[1,40]{1,0:T(1,128)S(1)}, f32[1,40]{1,0:T(1,128)}, u32[]{:S(2)}) copy-start(f32[1,40]{1,0:T(1,128)} %param.10) | copy-start | bytes 484
  64.7 20.9 %all-to-all-start.1 = ((bf16[4,40,1536]{2,1,0:T(8,128)(2,1)}), bf16[4,40,1536]{2,1,0:T(8,128)(2,1)S(1)}, u32[]{:S(2)}, u32[]{:S(2)}) async-start(bf16[4,40,1536]{2,1,0:T(8,128)(2,1)} %bitcast.11), calls=%async_computation.1 | async-start | bytes 983040 | tf_op jit(solution)/shard_map/all_to_all | solution.py:51

commit v8 on v7

--- a/solution.py
+++ b/solution.py
@@ -28,11 +28,10 @@
     halves = lam[0].reshape(hole_local // (PAIR * out_rows), PAIR, out_rows, part_local)
     half = (hole_local // PAIR, part_local)
     place = lax.axis_index("zl")
+    given = lax.dynamic_slice_in_dim(halves, 1 - place, 1, 1).reshape(half)
+    pair = lax.all_gather(given, "zl")
+    tile, pair, halves = lax.optimization_barrier((v_pppp[0], pair, halves))
     kept = lax.dynamic_slice_in_dim(halves, place, 1, 1).reshape(half)
-    given = lax.dynamic_slice_in_dim(halves, 1 - place, 1, 1).reshape(half)
-    kept, given = lax.optimization_barrier((kept, given))
-    pair = lax.all_gather(given, "zl")
-    tile, pair = lax.optimization_barrier((v_pppp[0], pair))
     taken = jnp.where(place == 1, pair[0], pair[1])
     other_tile = lax.ppermute(tile, "zl", swap)
     blocks = jnp.arange(hole_local // (PAIR * out_rows), dtype=jnp.int32)

time: 86.8 us -> 86.7 us (level)
    dynamic_slice x1, local copies, waits for them, and re-layouts: 0.97 us -> 0.01 us  [local(): given = lax.dynamic_slice_in_dim(halves, 1 - place, 1, 1).reshape(half)]
    unnamed x8 -> x10, local copies, waits for them, and re-layouts: 0.01 us -> 0.91 us
where the time goes in v8:
time: 86.7 us; the launch traced here: 86.4 us
  blocking collectives  54.6 us (63%)
  starting transfers between devices  13.4 us (15%)
  waiting for transfers between devices  11.4 us (13%)
  matrix products  2.35 us (3%)
  other arithmetic  2.23 us (3%)
  between operations  1.38 us (2%)
  local copies, waits for them, and re-layouts  1.04 us (1%)
    all_gather x1, blocking collectives, local(): left = lax.all_gather(both, 'row', axis=0, tiled=True)  26.8 us
    all_to_all x1, blocking collectives, local(): got = lax.all_to_all(part, 'x', 0, 0)  22.5 us
    all_to_all x1, waiting for transfers between devices, local(): lax.all_to_all(some.reshape(NZ // PAIR, out_rows, out_cols), 'zh', 0, 0)  11.4 us
    all_to_all x1, starting transfers between devices, local(): lax.all_to_all(some.reshape(NZ // PAIR, out_rows, out_cols), 'zh', 0, 0)  9.41 us
    all_gather x1, blocking collectives, local(): pair = lax.all_gather(given, 'zl')  5.21 us
    ppermute x1, starting transfers between devices, local(): other_tile = lax.ppermute(tile, 'zl', swap)  3.94 us
  transfers between devices with their start and end apart: 2, of which 1 were waited for; matrix products, arithmetic and copies ran while one was open for 2% of the time, Pallas kernels for 0%

profile of v8, /device:TPU:56, one launch (start us, length us, event | category | flops | bytes accessed | tf_op | source)
XLA Modules:
  0.0 86.4 jit_solution(16545227756160193329)
XLA Ops:
  0.0 0.0 copy-start
  0.0 0.0 copy-start.1
  0.0 0.9 %copy-done = bf16[1,160,384]{2,1,0:T(8,128)(2,1)S(1)} copy-done((bf16[1,160,384]{2,1,0:T(8,128)(2,1)S(1)}, bf16[1,160,384]{2,1,0:T(8,128)(2,1)}, u32[]{:S(2)}) %copy-start) | copy-done | bytes 122904
  0.9 5.2 %all_gather.6 = bf16[2,80,384]{2,1,0:T(8,128)(2,1)S(1)} all-gather(bf16[1,80,384]{2,1,0:T(8,128)(2,1)S(1)} %bitcast.26), channel_id=1, replica_groups=mesh['grp'=2,'row'=8,'x'=4,'zh'=4,'zl'=2] {'zl'}, dimensions={0}, use_global_device_ids=true | all-gather | bytes 184320 | tf_op jit(solution)/shard_map/all_gather | solution.py:32
  6.1 3.9 %collective-permute-start = (bf16[384,1536]{1,0:T(8,128)(2,1)}, bf16[384,1536]{1,0:T(8,128)(2,1)S(1)}, u32[]{:S(2)}, u32[]{:S(2)}) collective-permute-start(bf16[384,1536]{1,0:T(8,128)(2,1)} %bitcast.24), channel_id=1, source_target_pairs={{0,1},{1,0},{2,3},{3,2},{4,5},{5,4},{6,7},{7,6},{8,9},{9,8},{10,11... | collective-permute-start | bytes 3538952 | tf_op jit(solution)/shard_map/ppermute | solution.py:36
  10.7 0.1 add_multiply_fusion
  10.8 0.1 add_compare_fusion.1
  11.6 0.1 add_compare_fusion.2
  11.6 0.1 lt.60
  11.8 0.1 and_select_fusion
  11.9 26.8 %all_gather.7 = bf16[640,768]{1,0:T(8,128)(2,1)S(1)} all-gather(bf16[80,768]{1,0:T(8,128)(2,1)S(1)} %and_select_fusion), channel_id=1, replica_groups=mesh['grp'=2,'row'=8,'x'=4,'zh'=4,'zl'=2] {'row'}, dimensions={0}, use_global_device_ids=true | all-gather | bytes 1105920 | tf_op jit(solution)/shard_map/all_gather | solution.py:43
  38.7 0.0 copy-done.1
  38.7 1.2 %fusion.1 = f32[640,1536]{1,0:T(8,128)S(1)} fusion(bf16[384,1536]{1,0:T(8,128)(2,1)S(1)} %bitcast.25, bf16[640,768]{1,0:T(8,128)(2,1)S(1)} %all_gather.7), kind=kOutput, calls=%fused_computation.3 | convolution fusion | flops 754974720 | bytes 5603328 | tf_op jit(solution)/shard_map/dot_general | solution.py:44
  39.9 0.0 collective-permute-done
  39.9 1.2 %add_convert_fusion = bf16[640,1536]{1,0:T(8,128)(2,1)S(1)} fusion(f32[640,1536]{1,0:T(8,128)S(1)} %fusion.1, bf16[384,1536]{1,0:T(8,128)(2,1)S(1)} %collective-permute-done, bf16[640,768]{1,0:T(8,128)(2,1)S(1)} %all_gather.7), kind=kOutput, calls=%fused_computation | convolution fusion | flops 756940800 | bytes 7569408 | tf_op jit(solution)/shard_map/dot_general | solution.py:45
  41.1 22.5 %all_to_all.10 = bf16[4,160,1536]{2,1,0:T(8,128)(2,1)S(1)} all-to-all(bf16[4,160,1536]{2,1,0:T(8,128)(2,1)S(1)} %bitcast.23), channel_id=1, replica_groups=mesh['grp'=2,'row'=8,'x'=4,'zh'=4,'zl'=2] {'x'}, dimensions={0} | all-to-all | bytes 3932160 | tf_op jit(solution)/shard_map/all_to_all | solution.py:48
  63.6 0.0 copy-start.3
  63.6 0.0 copy-start.2
  63.6 0.0 copy-start.4
  63.6 1.0 %add_convert_fusion.1 = bf16[1,160,1536]{2,1,0:T(8,128)(2,1)} fusion(bf16[4,160,1536]{2,1,0:T(8,128)(2,1)S(1)} %all_to_all.10), kind=kLoop, calls=%fused_computation.1 | loop fusion | flops 1966080 | bytes 2457600 | tf_op jit(solution)/shard_map/convert
  64.6 9.4 %all-to-all-start.1 = ((bf16[4,40,1536]{2,1,0:T(8,128)(2,1)}), bf16[4,40,1536]{2,1,0:T(8,128)(2,1)S(1)}, u32[]{:S(2)}, u32[]{:S(2)}) async-start(bf16[4,40,1536]{2,1,0:T(8,128)(2,1)} %bitcast.10), calls=%async_computation.1 | async-start | bytes 983040 | tf_op jit(solution)/shard_map/all_to_all | solution.py:50
  74.0 0.0 copy-done.3
  74.1 11.4 %all-to-all-done.1 = bf16[4,40,1536]{2,1,0:T(8,128)(2,1)S(1)} async-done(((bf16[4,40,1536]{2,1,0:T(8,128)(2,1)}), bf16[4,40,1536]{2,1,0:T(8,128)(2,1)S(1)}, u32[]{:S(2)}, u32[]{:S(2)}) %all-to-all-start.1) | async-done | bytes 491552 | tf_op jit(solution)/shard_map/all_to_all | solution.py:50
  85.5 0.0 copy-done.2
  85.5 0.0 copy-done.4
  85.5 0.8 select_convert_fusion
  (8 shorter events, 0.1 us)
Async XLA Ops:
  0.0 0.9 %copy-start = (bf16[1,160,384]{2,1,0:T(8,128)(2,1)S(1)}, bf16[1,160,384]{2,1,0:T(8,128)(2,1)}, u32[]{:S(2)}) copy-start(bf16[1,160,384]{2,1,0:T(8,128)(2,1)} %param.8) | copy-start | bytes 368644
  0.0 38.7 %copy-start.1 = (bf16[1,384,1536]{2,1,0:T(8,128)(2,1)S(1)}, bf16[1,384,1536]{2,1,0:T(8,128)(2,1)}, u32[]{:S(2)}) copy-start(bf16[1,384,1536]{2,1,0:T(8,128)(2,1)} %param.7) | copy-start | bytes 3538948
  6.1 33.8 %collective-permute-start = (bf16[384,1536]{1,0:T(8,128)(2,1)}, bf16[384,1536]{1,0:T(8,128)(2,1)S(1)}, u32[]{:S(2)}, u32[]{:S(2)}) collective-permute-start(bf16[384,1536]{1,0:T(8,128)(2,1)} %bitcast.24), channel_id=1, source_target_pairs={{0,1},{1,0},{2,3},{3,2},{4,5},{5,4},{6,7},{7,6},{8,9},{9,8},{10,11... | collective-permute-start | bytes 3538952 | tf_op jit(solution)/shard_map/ppermute | solution.py:36
  63.6 10.4 %copy-start.3 = (f32[1,1536]{1,0:T(1,128)S(1)}, f32[1,1536]{1,0:T(1,128)}, u32[]{:S(2)}) copy-start(f32[1,1536]{1,0:T(1,128)} %param.11) | copy-start | bytes 18436
  63.6 21.9 %copy-start.2 = (bf16[1,40,1536]{2,1,0:T(8,128)(2,1)S(1)}, bf16[1,40,1536]{2,1,0:T(8,128)(2,1)}, u32[]{:S(2)}) copy-start(bf16[1,40,1536]{2,1,0:T(8,128)(2,1)} %param.9) | copy-start | bytes 368644
  63.6 21.9 %copy-start.4 = (f32[1,40]{1,0:T(1,128)S(1)}, f32[1,40]{1,0:T(1,128)}, u32[]{:S(2)}) copy-start(f32[1,40]{1,0:T(1,128)} %param.10) | copy-start | bytes 484
  64.6 20.9 %all-to-all-start.1 = ((bf16[4,40,1536]{2,1,0:T(8,128)(2,1)}), bf16[4,40,1536]{2,1,0:T(8,128)(2,1)S(1)}, u32[]{:S(2)}, u32[]{:S(2)}) async-start(bf16[4,40,1536]{2,1,0:T(8,128)(2,1)} %bitcast.10), calls=%async_computation.1 | async-start | bytes 983040 | tf_op jit(solution)/shard_map/all_to_all | solution.py:50

commit v9 on v7

--- a/solution.py
+++ b/solution.py
@@ -34,7 +34,8 @@
     pair = lax.all_gather(given, "zl")
     tile, pair = lax.optimization_barrier((v_pppp[0], pair))
     taken = jnp.where(place == 1, pair[0], pair[1])
-    other_tile = lax.ppermute(tile, "zl", swap)
+    upper = lax.ppermute(tile[: part_local // 2], "zl", swap)
+    lower = lax.ppermute(tile[part_local // 2 :], "zl", swap)
     blocks = jnp.arange(hole_local // (PAIR * out_rows), dtype=jnp.int32)
     hole_ids = y * hole_local + (blocks[:, None] * PAIR + place) * out_rows + jnp.arange(out_rows, dtype=jnp.int32)
     part_ids = jnp.stack([col, col + 1 - 2 * place])[:, None] * part_local + jnp.arange(part_local, dtype=jnp.int32)
@@ -43,7 +44,7 @@
     both = jnp.where(keep, both, jnp.zeros_like(both))
     left = lax.all_gather(both, "row", axis=0, tiled=True)
     part = jnp.dot(left[:, :part_local], tile, preferred_element_type=jnp.float32)
-    part = part + jnp.dot(left[:, part_local:], other_tile, preferred_element_type=jnp.float32)
+    part = part + jnp.dot(left[:, part_local:], jnp.concatenate([upper, lower], axis=0), preferred_element_type=jnp.float32)
 
     part = part.astype(jnp.bfloat16).reshape(NX, NZ // PAIR * out_rows, out_cols)
     got = lax.all_to_all(part, "x", 0, 0)

time: 86.8 us -> 94 us (1.083); the launches traced: 86.4 us -> 92.2 us
  local copies, waits for them, and re-layouts: 1.09 us -> 3.03 us
  starting transfers between devices: 13.3 us -> 15.2 us
  other arithmetic: 2.23 us -> 3.91 us
    ppermute x1 -> x2, starting transfers between devices: 3.94 us -> 5.88 us  [the longest x1 3.96 us: local(): upper = lax.ppermute(tile[:part_local // 2], 'zl', swap)]
    all_to_all x1, blocking collectives: 22.5 us -> 21 us  [local(): got = lax.all_to_all(part, 'x', 0, 0)]
    all_gather x1, blocking collectives: 26.8 us -> 28.3 us  [local(): left = lax.all_gather(both, 'row', axis=0, tiled=True)]
    slice x0 -> x1, local copies, waits for them, and re-layouts: none -> 1.42 us  [local(): upper = lax.ppermute(tile[:part_local // 2], 'zl', swap)]
  transfers between devices with their start and end apart: 2 -> 3, of which waited for: 1 -> 1; matrix products, arithmetic and copies ran while one was open for 2% -> 4% of each run, Pallas kernels for 0% -> 0%
where the time goes in v9:
time: 94 us; the launch traced here: 92.2 us
  blocking collectives  54.7 us (58%)
  starting transfers between devices  15.2 us (16%)
  waiting for transfers between devices  11.6 us (12%)
  other arithmetic  3.91 us (4%)
  local copies, waits for them, and re-layouts  3.03 us (3%)
  matrix products  2.37 us (3%)
  between operations  1.39 us (1%)
    all_gather x1, blocking collectives, local(): left = lax.all_gather(both, 'row', axis=0, tiled=True)  28.3 us
    all_to_all x1, blocking collectives, local(): got = lax.all_to_all(part, 'x', 0, 0)  21 us
    all_to_all x1, waiting for transfers between devices, local(): lax.all_to_all(some.reshape(NZ // PAIR, out_rows, out_cols), 'zh', 0, 0)  11.6 us
    all_to_all x1, starting transfers between devices, local(): lax.all_to_all(some.reshape(NZ // PAIR, out_rows, out_cols), 'zh', 0, 0)  9.36 us
    all_gather x1, blocking collectives, local(): pair = lax.all_gather(given, 'zl')  5.32 us
    ppermute x1, starting transfers between devices, local(): upper = lax.ppermute(tile[:part_local // 2], 'zl', swap)  3.96 us
    ppermute x1, starting transfers between devices, local(): lower = lax.ppermute(tile[part_local // 2:], 'zl', swap)  1.92 us
  transfers between devices with their start and end apart: 3, of which 1 were waited for; matrix products, arithmetic and copies ran while one was open for 4% of the time, Pallas kernels for 0%

profile of v9, /device:TPU:56, one launch (start us, length us, event | category | flops | bytes accessed | tf_op | source)
XLA Modules:
  0.0 92.2 jit_solution(217273265654428116)
XLA Ops:
  0.0 1.5 %constant_dynamic-slice_fusion = (bf16[2,1,40,384]{3,2,1,0:T(8,128)(2,1)S(1)}, bf16[2,1,40,384]{3,2,1,0:T(8,128)(2,1)}) fusion(bf16[2,2,40,384]{3,2,1,0:T(8,128)(2,1)} %bitcast.25, s32[]{:T(128)S(6)} %select_n.27, s32[]{:T(128)S(6)} %select_n.26), kind=kLoop, calls=%fused_computation.15 | loop fusion | bytes 245768 | tf_op jit(solution)/shard_map/dynamic_slice | solution.py:32
  1.5 5.3 %all-gather = bf16[160,384]{1,0:T(8,128)(2,1)} all-gather(bf16[80,384]{1,0:T(8,128)(2,1)S(1)} %bitcast.23), channel_id=2, replica_groups=mesh['grp'=2,'row'=8,'x'=4,'zh'=4,'zl'=2] {'zl'}, dimensions={0}, use_global_device_ids=true | all-gather | bytes 184320 | tf_op jit(solution)/shard_map/all_gather | solution.py:34
  6.8 0.0 copy-start
  6.8 1.4 %fusion.7 = (bf16[192,1536]{1,0:T(8,128)(2,1)S(1)}, bf16[192,1536]{1,0:T(8,128)(2,1)S(1)}) fusion(bf16[384,1536]{1,0:T(8,128)(2,1)} %bitcast.20), kind=kLoop, calls=%fused_computation.20 | loop fusion | bytes 2359296 | tf_op jit(solution)/shard_map/slice | solution.py:37
  8.2 4.0 %collective-permute-start = (bf16[192,1536]{1,0:T(8,128)(2,1)S(1)}, bf16[192,1536]{1,0:T(8,128)(2,1)S(1)}, u32[]{:S(2)}, u32[]{:S(2)}) collective-permute-start(bf16[192,1536]{1,0:T(8,128)(2,1)S(1)} %get-tuple-element.13), channel_id=1, source_target_pairs={{0,1},{1,0},{2,3},{3,2},{4,5},{5,4},{6,7},{7,6},{8,9},{9,8},{10,11... | collective-permute-start | bytes 1769480 | tf_op jit(solution)/shard_map/ppermute | solution.py:37
  12.2 1.9 %collective-permute-start.1 = (bf16[192,1536]{1,0:T(8,128)(2,1)S(1)}, bf16[192,1536]{1,0:T(8,128)(2,1)S(1)}, u32[]{:S(2)}, u32[]{:S(2)}) collective-permute-start(bf16[192,1536]{1,0:T(8,128)(2,1)S(1)} %get-tuple-element.14), channel_id=1, source_target_pairs={{0,1},{1,0},{2,3},{3,2},{4,5},{5,4},{6,7},{7,6},{8,9},{9,8},{10,11... | collective-permute-start | bytes 1769480 | tf_op jit(solution)/shard_map/ppermute | solution.py:38
  14.8 0.1 add_multiply_fusion
  14.9 0.1 add_compare_fusion.1
  15.6 0.1 add_compare_fusion.2
  15.7 0.1 lt.60
  15.8 0.9 select_bitcast_fusion
  16.7 0.9 %and_select_fusion = bf16[80,768]{1,0:T(8,128)(2,1)S(1)} fusion(bf16[80,384]{1,0:T(8,128)(2,1)S(1)} %select_bitcast_fusion, bf16[80,384]{1,0:T(8,128)(2,1)} %bitcast.24, pred[768]{0:T(1024)(128)(4,1)S(1)} %lt.63, pred[80]{0:T(512)(128)(4,1)S(1)} %lt.60), kind=kLoop, calls=%fused_computation.9 | loop fusion | flops 368640 | bytes 246608 | tf_op jit(solution)/shard_map/jit(_where)/select_n | solution.py:44
  17.6 28.3 %all_gather.11 = bf16[640,768]{1,0:T(8,128)(2,1)S(1)} all-gather(bf16[80,768]{1,0:T(8,128)(2,1)S(1)} %and_select_fusion), channel_id=1, replica_groups=mesh['grp'=2,'row'=8,'x'=4,'zh'=4,'zl'=2] {'row'}, dimensions={0}, use_global_device_ids=true | all-gather | bytes 1105920 | tf_op jit(solution)/shard_map/all_gather | solution.py:45
  45.9 0.0 copy-done
  45.9 1.2 %fusion.4 = f32[640,1536]{1,0:T(8,128)S(1)} fusion(bf16[384,1536]{1,0:T(8,128)(2,1)S(1)} %bitcast.21, bf16[640,768]{1,0:T(8,128)(2,1)S(1)} %all_gather.11), kind=kOutput, calls=%fused_computation.6 | convolution fusion | flops 754974720 | bytes 5603328 | tf_op jit(solution)/shard_map/dot_general | solution.py:46
  47.1 0.0 collective-permute-done
  47.1 0.0 collective-permute-done.1
  47.1 1.2 %add_convert_fusion = bf16[640,1536]{1,0:T(8,128)(2,1)S(1)} fusion(f32[640,1536]{1,0:T(8,128)S(1)} %fusion.4, bf16[192,1536]{1,0:T(8,128)(2,1)S(1)} %collective-permute-done.1, bf16[192,1536]{1,0:T(8,128)(2,1)S(1)} %collective-permute-done, bf16[640,768]{1,0:T(8,128)(2,1)S(1)} %all_gather.11), kind=kOutput, calls=%fused_computation | convolution fusion | flops 759300096 | bytes 7569408 | tf_op jit(solution)/shard_map/dot_general | solution.py:47
  48.3 21.0 %all_to_all.10 = bf16[4,160,1536]{2,1,0:T(8,128)(2,1)S(1)} all-to-all(bf16[4,160,1536]{2,1,0:T(8,128)(2,1)S(1)} %bitcast.19), channel_id=1, replica_groups=mesh['grp'=2,'row'=8,'x'=4,'zh'=4,'zl'=2] {'x'}, dimensions={0} | all-to-all | bytes 3932160 | tf_op jit(solution)/shard_map/all_to_all | solution.py:50
  69.4 0.0 copy-start.2
  69.4 0.0 copy-start.1
  69.4 0.0 copy-start.3
  69.4 1.0 %add_convert_fusion.1 = bf16[1,160,1536]{2,1,0:T(8,128)(2,1)} fusion(bf16[4,160,1536]{2,1,0:T(8,128)(2,1)S(1)} %all_to_all.10), kind=kLoop, calls=%fused_computation.4 | loop fusion | flops 1966080 | bytes 2457600 | tf_op jit(solution)/shard_map/convert
  70.4 9.4 %all-to-all-start.1 = ((bf16[4,40,1536]{2,1,0:T(8,128)(2,1)}), bf16[4,40,1536]{2,1,0:T(8,128)(2,1)S(1)}, u32[]{:S(2)}, u32[]{:S(2)}) async-start(bf16[4,40,1536]{2,1,0:T(8,128)(2,1)} %bitcast.11), calls=%async_computation.1 | async-start | bytes 983040 | tf_op jit(solution)/shard_map/all_to_all | solution.py:52
  79.7 0.0 copy-done.2
  79.8 11.6 %all-to-all-done.1 = bf16[4,40,1536]{2,1,0:T(8,128)(2,1)S(1)} async-done(((bf16[4,40,1536]{2,1,0:T(8,128)(2,1)}), bf16[4,40,1536]{2,1,0:T(8,128)(2,1)S(1)}, u32[]{:S(2)}, u32[]{:S(2)}) %all-to-all-start.1) | async-done | bytes 491552 | tf_op jit(solution)/shard_map/all_to_all | solution.py:52
  91.4 0.0 copy-done.1
  91.4 0.0 copy-done.3
  91.4 0.8 select_convert_fusion
  (5 shorter events, 0.1 us)
Async XLA Ops:
  6.8 39.1 %copy-start = (bf16[1,384,1536]{2,1,0:T(8,128)(2,1)S(1)}, bf16[1,384,1536]{2,1,0:T(8,128)(2,1)}, u32[]{:S(2)}) copy-start(bf16[1,384,1536]{2,1,0:T(8,128)(2,1)} %param.7) | copy-start | bytes 3538948
  8.2 38.9 %collective-permute-start = (bf16[192,1536]{1,0:T(8,128)(2,1)S(1)}, bf16[192,1536]{1,0:T(8,128)(2,1)S(1)}, u32[]{:S(2)}, u32[]{:S(2)}) collective-permute-start(bf16[192,1536]{1,0:T(8,128)(2,1)S(1)} %get-tuple-element.13), channel_id=1, source_target_pairs={{0,1},{1,0},{2,3},{3,2},{4,5},{5,4},{6,7},{7,6},{8,9},{9,8},{10,11... | collective-permute-start | bytes 1769480 | tf_op jit(solution)/shard_map/ppermute | solution.py:37
  12.2 34.9 %collective-permute-start.1 = (bf16[192,1536]{1,0:T(8,128)(2,1)S(1)}, bf16[192,1536]{1,0:T(8,128)(2,1)S(1)}, u32[]{:S(2)}, u32[]{:S(2)}) collective-permute-start(bf16[192,1536]{1,0:T(8,128)(2,1)S(1)} %get-tuple-element.14), channel_id=1, source_target_pairs={{0,1},{1,0},{2,3},{3,2},{4,5},{5,4},{6,7},{7,6},{8,9},{9,8},{10,11... | collective-permute-start | bytes 1769480 | tf_op jit(solution)/shard_map/ppermute | solution.py:38
  69.4 10.4 %copy-start.2 = (f32[1,1536]{1,0:T(1,128)S(1)}, f32[1,1536]{1,0:T(1,128)}, u32[]{:S(2)}) copy-start(f32[1,1536]{1,0:T(1,128)} %param.11) | copy-start | bytes 18436
  69.4 22.0 %copy-start.1 = (bf16[1,40,1536]{2,1,0:T(8,128)(2,1)S(1)}, bf16[1,40,1536]{2,1,0:T(8,128)(2,1)}, u32[]{:S(2)}) copy-start(bf16[1,40,1536]{2,1,0:T(8,128)(2,1)} %param.9) | copy-start | bytes 368644
  69.4 22.0 %copy-start.3 = (f32[1,40]{1,0:T(1,128)S(1)}, f32[1,40]{1,0:T(1,128)}, u32[]{:S(2)}) copy-start(f32[1,40]{1,0:T(1,128)} %param.10) | copy-start | bytes 484
  70.4 21.0 %all-to-all-start.1 = ((bf16[4,40,1536]{2,1,0:T(8,128)(2,1)}), bf16[4,40,1536]{2,1,0:T(8,128)(2,1)S(1)}, u32[]{:S(2)}, u32[]{:S(2)}) async-start(bf16[4,40,1536]{2,1,0:T(8,128)(2,1)} %bitcast.11), calls=%async_computation.1 | async-start | bytes 983040 | tf_op jit(solution)/shard_map/all_to_all | solution.py:52
